TPU v7x, 32 devices: a whole 2x2x4 slice. The times are simulated.
32 devices in a mesh: tok: 8 (over z, x), hd: 4 (over y, core).
Axes of the slice: x: 2, y: 2, z: 4, core: 2. Of those that a mesh axis runs over, the one named last changes fastest.
Arguments:
- residual_in: bfloat16 [2048, 2048], P('tok'), may hold values from -6 to 6
- queries: bfloat16 [2048, 2048], P('tok', 'hd'), may hold values from -11 to 11
- keys: bfloat16 [2048, 2048], P('tok', 'hd'), may hold values from -11 to 11
- values: bfloat16 [2048, 2048], P('tok', 'hd'), may hold values from -12 to 12
- segment_ids: int32 [2048], replicated, may hold values from 0 to 3, never falling along the last dimension, each value on 1 to 1024 neighbouring positions
- out_proj: bfloat16 [2048, 2048], P('hd'), may hold values from -0.125 to 0.125
- norm_gain: float32 [2048], replicated, may hold values from 0.1 to 1.9
- shared_gate: bfloat16 [2048, 2816], P(None, 'hd'), may hold values from -0.125 to 0.125
- shared_up: bfloat16 [2048, 2816], P(None, 'hd'), may hold values from -0.125 to 0.125
- shared_down: bfloat16 [2816, 2048], P('hd'), may hold values from -0.109375 to 0.109375
- expert_gate: bfloat16 [2048, 90112], P(None, ('tok', 'hd')), may hold values from -0.125 to 0.125
- expert_up: bfloat16 [2048, 90112], P(None, ('tok', 'hd')), may hold values from -0.125 to 0.125
- expert_down: bfloat16 [90112, 2048], P(('tok', 'hd')), may hold values from -0.15625 to 0.15625
- expert_ids: int32 [2048, 6], P('tok'), may hold values from 0 to 63, all different within a row; in each aligned block of 256 rows (0 to 255, 256 to 511, ...) at most 48 rows name the same one
- route_weight: float32 [2048, 6], P('tok'), may hold values from 0.05 to 0.4
- block_table: int32 [128], P('tok'), may hold values from 0 to 127, as said below
Outputs:
- output: bfloat16 [2048, 2048], P(('tok', 'hd'))
- kv_cache: bfloat16 [128, 16, 4096], P('tok', None, 'hd')
Inputs may be any that keep to these rules, and one draw needn't show every extreme that they name: `segment_ids`: never falling; each prompt has 1 to 1024 tokens, one exactly 1024. `expert_ids`: each row names 6 different experts; in each aligned block of 256 rows (the rows of one index of tok) no expert is named by more than 48 rows, a bound that some block reaches. `block_table`: each aligned run of 16 entries is a permutation of its own index range.
All inputs are finite; a program needn't handle non-finite values.
Results may differ from a plain program's by a relative error of at most 0.02.
Values may be sent and summed in bfloat16 or wider, within the bound.
No kernel may reach another device: no remote copies, remote signals or barrier semaphores. Data moves between devices by JAX's collectives and lax.ppermute only.
A program may use at most 128 MiB of HBM per device.

v0:
```python
import math

import jax
import jax.numpy as jnp
import numpy as np
from jax import lax
from jax.experimental import pallas as pl
from jax.experimental.pallas import tpu as pltpu
from jax.sharding import PartitionSpec as P

HD = 128
EXPERTS = 64
FF_E = 1408
PAGE = 16
CAP = 48


MASKED_SCORE = -1e30
NORM_EPSILON = 1e-06


def from_behind(array, axis, by):
    length = lax.axis_size(axis)
    pairs = [(i, i + by) for i in range(length) if 0 <= i + by < length]
    return lax.ppermute(array, axis, pairs)


def rms_normed(resid_state, norm_gain):
    mean_square = jnp.mean(resid_state * resid_state, axis=1, keepdims=True)
    return (resid_state * lax.rsqrt(mean_square + NORM_EPSILON) * norm_gain).astype(jnp.bfloat16)


def general_body(
    residual_in,
    queries,
    keys,
    values,
    segment_ids,
    out_proj,
    norm_gain,
    shared_gate,
    shared_up,
    shared_down,
    expert_gate,
    expert_up,
    expert_down,
    expert_ids,
    route_weight,
    block_table,
):
    block_len = residual_in.shape[0]
    model_width = residual_in.shape[1]
    tok_count = lax.axis_size("tok")
    hd_count = lax.axis_size("hd")
    tok_here = lax.axis_index("tok")
    hd_here = lax.axis_index("hd")
    heads_here = queries.shape[1] // HD
    query_three = queries.reshape(block_len, heads_here, HD)
    offsets = lax.iota(jnp.int32, block_len)
    query_pos = tok_here * block_len + offsets
    query_seg = lax.dynamic_slice_in_dim(segment_ids, tok_here * block_len, block_len, 0)

    def attend(carried, key_blk, value_blk, source):
        safe_source = jnp.maximum(source, 0)
        key_seg = lax.dynamic_slice_in_dim(segment_ids, safe_source * block_len, block_len, 0)
        key_pos = source * block_len + offsets

        def compute(current):
            running_max, denom_sum, weighted_sum = current
            scores = jnp.einsum(
                "qhd,khd->hqk",
                query_three,
                key_blk.reshape(block_len, heads_here, HD),
                preferred_element_type=jnp.float32,
            ) / math.sqrt(HD)
            allowed = (key_seg[None, :] == query_seg[:, None]) & (
                key_pos[None, :] <= query_pos[:, None]
            )
            scores = jnp.where(allowed[None], scores, MASKED_SCORE)
            new_max = jnp.maximum(running_max, jnp.max(scores, axis=2))
            shrink = jnp.exp(running_max - new_max)
            exp_scores = jnp.where(allowed[None], jnp.exp(scores - new_max[:, :, None]), 0.0)
            denom_sum = denom_sum * shrink + jnp.sum(exp_scores, axis=2)
            update = jnp.einsum(
                "hqk,khd->qhd",
                exp_scores.astype(jnp.bfloat16),
                value_blk.reshape(block_len, heads_here, HD),
                preferred_element_type=jnp.float32,
            )
            weighted_sum = weighted_sum * jnp.transpose(shrink)[:, :, None] + update
            return (new_max, denom_sum, weighted_sum)

        is_live = (source >= 0) & (
            segment_ids[safe_source * block_len + block_len - 1] >= query_seg[0]
        )
        return lax.cond(is_live, compute, lambda unchanged: unchanged, carried)

    initial = (
        jnp.full((heads_here, block_len), MASKED_SCORE, jnp.float32),
        jnp.zeros((heads_here, block_len), jnp.float32),
        jnp.zeros((block_len, heads_here, HD), jnp.float32),
    )
    carried = attend(initial, keys, values, tok_here)

    def relay(relay_step, loop_carry):
        moving, inner_state = loop_carry
        moving = from_behind(moving, "tok", 1)
        inner_state = attend(inner_state, moving[0], moving[1], tok_here - relay_step - 1)
        return (moving, inner_state)

    _, final_state = lax.fori_loop(0, tok_count // 2, relay, (jnp.stack([keys, values]), carried))
    weighted_sum = final_state[2]
    denom_sum = final_state[1]
    attended = (
        (weighted_sum / jnp.transpose(denom_sum)[:, :, None])
        .astype(jnp.bfloat16)
        .reshape(block_len, heads_here * HD)
    )
    row_count = block_len // hd_count
    row_start = hd_here * row_count
    head_terms = jnp.dot(attended, out_proj, preferred_element_type=jnp.float32)
    resid_full = residual_in.astype(jnp.float32) + lax.psum(
        head_terms.astype(jnp.bfloat16), "hd"
    ).astype(jnp.float32)
    normed = rms_normed(resid_full, norm_gain)
    resid_rows = lax.dynamic_slice_in_dim(resid_full, row_start, row_count, 0)
    shared_gate_val = jnp.dot(normed, shared_gate, preferred_element_type=jnp.float32)
    shared_up_val = jnp.dot(normed, shared_up, preferred_element_type=jnp.float32)
    shared_hidden = (jax.nn.silu(shared_gate_val) * shared_up_val).astype(jnp.bfloat16)
    partial_out = jnp.dot(shared_hidden, shared_down, preferred_element_type=jnp.float32)
    slice_width = expert_gate.shape[1]
    held_count = max(1, slice_width // FF_E)
    part_width = slice_width // held_count
    per_group = slice_width * hd_count // FF_E
    first_local = hd_here * slice_width // FF_E
    expert_range = lax.iota(jnp.int32, EXPERTS)
    onehot = jnp.sum(
        (expert_ids[:, :, None] == expert_range[None, None, :]).astype(jnp.int32), axis=1
    )
    earlier = jnp.cumsum(onehot, axis=0) - onehot
    slot_index = jnp.take_along_axis(earlier, expert_ids, axis=1)
    flat_expert = expert_ids.reshape(-1)
    flat_slot = slot_index.reshape(-1)
    row_source = jnp.repeat(offsets, expert_ids.shape[1])
    row_table = (
        jnp.full((EXPERTS, CAP), block_len, jnp.int32).at[flat_expert, flat_slot].set(row_source)
    )
    weight_table = (
        jnp.zeros((EXPERTS, CAP), jnp.float32)
        .at[flat_expert, flat_slot]
        .set(route_weight.reshape(-1))
    )
    send_rows = lax.dynamic_slice_in_dim(
        row_table.reshape(tok_count, per_group, CAP), first_local, held_count, 1
    )
    send_weight = lax.dynamic_slice_in_dim(
        weight_table.reshape(tok_count, per_group, CAP), first_local, held_count, 1
    )
    padded_rows = jnp.concatenate([normed, jnp.zeros((1, model_width), jnp.bfloat16)], axis=0)
    outgoing = padded_rows[send_rows]
    gate_three = expert_gate.reshape(model_width, held_count, part_width)
    up_three = expert_up.reshape(model_width, held_count, part_width)
    down_three = expert_down.reshape(held_count, part_width, model_width)
    incoming = lax.all_to_all(outgoing, "tok", split_axis=0, concat_axis=0, tiled=True)
    gate_val = jnp.einsum(
        "secd,def->secf", incoming, gate_three, preferred_element_type=jnp.float32
    )
    up_val = jnp.einsum("secd,def->secf", incoming, up_three, preferred_element_type=jnp.float32)
    hidden = (jax.nn.silu(gate_val) * up_val).astype(jnp.bfloat16)
    result = jnp.einsum(
        "secf,efd->secd", hidden, down_three, preferred_element_type=jnp.float32
    ).astype(jnp.bfloat16)
    returned_rows = lax.all_to_all(result, "tok", split_axis=0, concat_axis=0, tiled=True)
    weighted_rows = returned_rows.astype(jnp.float32) * send_weight[:, :, :, None]
    routed = (
        jnp.zeros((block_len + 1, model_width), jnp.float32)
        .at[send_rows.reshape(-1)]
        .add(weighted_rows.reshape(-1, model_width))[:block_len]
    )
    summed_rows = lax.psum_scatter(
        (partial_out + routed).astype(jnp.bfloat16), "hd", scatter_dimension=0, tiled=True
    ).astype(jnp.float32)
    output = (resid_rows + summed_rows).astype(jnp.bfloat16)
    page_count = block_len // PAGE
    page_data = jnp.stack(
        [keys.reshape(block_len, heads_here, HD), values.reshape(block_len, heads_here, HD)], axis=2
    )
    page_data = page_data.reshape(page_count, PAGE, heads_here * 2 * HD)
    local_pages = block_table - tok_here * page_count
    kv_pages = jnp.zeros_like(page_data).at[local_pages].set(page_data)
    return (output, kv_pages)


NZ = 4
BOTH = ("tok", "hd")
ROWS = 64
BLOCK = 256
GROUP_ROWS = 1024
SLOTS = 4 * CAP
NEXT_Z = {0: 1, 1: 3, 3: 2, 2: 0}
BACK_Z = {after: before for before, after in NEXT_Z.items()}
DEVICES = [(z, x, y, c) for z in range(NZ) for x in range(2) for y in range(2) for c in range(2)]


def flat_index(z, x, y, c):
    return (z * 2 + x) * 4 + y * 2 + c


def pairs_of(target):
    return [(flat_index(*device), flat_index(*target(*device))) for device in DEVICES]


Z_ON = pairs_of(lambda z, x, y, c: (NEXT_Z[z], x, y, c))
Z_BACK = pairs_of(lambda z, x, y, c: (BACK_Z[z], x, y, c))
Z_TWO = pairs_of(lambda z, x, y, c: (NEXT_Z[NEXT_Z[z]], x, y, c))
CORE_SWAP = pairs_of(lambda z, x, y, c: (z, x, y, 1 - c))
X_SWAP = pairs_of(lambda z, x, y, c: (z, 1 - x, y, c))
Y_SWAP = pairs_of(lambda z, x, y, c: (z, x, 1 - y, c))
X_THEN_Y = pairs_of(lambda z, x, y, c: (z, 1 - x, y, c) if c == 0 else (z, x, 1 - y, c))
Y_THEN_X = pairs_of(lambda z, x, y, c: (z, x, 1 - y, c) if c == 0 else (z, 1 - x, y, c))


def slice_order():
    order = np.zeros((4, 2, 16), np.int32)
    for y in range(2):
        for c in range(2):
            mine = {
                0: [(1, y, 0), (1, y, 1), (1, 1 - y, 0)],
                1: [(0, 1 - y, 1), (0, 1 - y, 0), (1, 1 - y, 1)],
            }
            places = [(0, y, c), (0, y, 1 - c)] + mine[c] + mine[1 - c]
            for group in range(2):
                order[y * 2 + c, group] = [
                    ((2 * group + part) * 2 + other) * 4 + at_y * 2 + at_c
                    for other, at_y, at_c in places
                    for part in range(2)
                ]
    return order


def send(array, pairs):
    return lax.ppermute(array, BOTH, pairs)


def added(first, second):
    return (first.astype(jnp.float32) + second.astype(jnp.float32)).astype(jnp.bfloat16)


def whole(space=pltpu.VMEM):
    return pl.BlockSpec(memory_space=space)


def pages_kernel(table, keys, values, joined, pages):
    heads = keys.shape[1] // HD
    for head in range(heads):
        lanes = slice(head * HD, (head + 1) * HD)
        joined[:, 2 * head * HD : (2 * head + 1) * HD] = keys[:, lanes]
        joined[:, (2 * head + 1) * HD : (2 * head + 2) * HD] = values[:, lanes]
    for page in range(keys.shape[0] // PAGE):
        pages[table[page]] = joined[page * PAGE : (page + 1) * PAGE, :]


def write_pages(keys, values, local_pages):
    rows, width = keys.shape
    return pl.pallas_call(
        pages_kernel,
        out_shape=(
            jax.ShapeDtypeStruct((rows, 2 * width), keys.dtype),
            jax.ShapeDtypeStruct((rows // PAGE, PAGE, 2 * width), keys.dtype),
        ),
        in_specs=[whole(pltpu.SMEM), whole(), whole()],
        out_specs=(whole(), whole()),
    )(local_pages, keys, values)


HEADS_HERE = 4


def attend_block(segments, query_segment, queries, block, source, diagonal, top, total, mixed):
    allowed = segments[pl.ds(source, 1), :] == query_segment[...]
    if diagonal:
        rows = lax.broadcasted_iota(jnp.int32, (BLOCK, BLOCK), 0)
        columns = lax.broadcasted_iota(jnp.int32, (BLOCK, BLOCK), 1)
        allowed = allowed & (columns <= rows)
    for head in range(HEADS_HERE):
        lane = slice(head, head + 1)
        key = block[:, 2 * head * HD : (2 * head + 1) * HD]
        value = block[:, (2 * head + 1) * HD : (2 * head + 2) * HD]
        scores = lax.dot_general(
            queries[:, head * HD : (head + 1) * HD],
            key,
            (((1,), (1,)), ((), ())),
            preferred_element_type=jnp.float32,
        ) * (1.0 / math.sqrt(HD))
        scores = jnp.where(allowed, scores, MASKED_SCORE)
        largest = jnp.max(scores, axis=1, keepdims=True)
        if not diagonal:
            before = top[:, lane]
            largest = jnp.maximum(largest, before)
        exp_scores = jnp.exp(scores - largest)
        update = jnp.dot(exp_scores.astype(jnp.bfloat16), value, preferred_element_type=jnp.float32)
        added_up = jnp.sum(exp_scores, axis=1, keepdims=True)
        if not diagonal:
            shrink = jnp.exp(before - largest)
            added_up += total[:, lane] * shrink
            update += mixed[head] * shrink
        top[:, lane] = largest
        total[:, lane] = added_up
        mixed[head] = update


def attend_earlier(place, segment_list, segments, query_segment, queries, blocks, top, total, mixed):
    for block, source in blocks:
        safe = jnp.maximum(source, 0)
        live = (source >= 0) & (
            segment_list[safe * BLOCK + BLOCK - 1] == segment_list[place[0] * BLOCK]
        )

        @pl.when(live)
        def _():
            attend_block(
                segments, query_segment, queries, block, safe, False, top, total, mixed
            )


def attention_first(
    place, segment_list, segments, query_segment, queries, own, near_x, near_z, top, total, mixed
):
    here = place[0]
    top[...] = jnp.zeros_like(top)
    total[...] = jnp.ones_like(total)
    attend_block(segments, query_segment, queries, own, here, True, top, total, mixed)
    odd = here % 2
    blocks = [(near_x, jnp.where(odd == 1, here - 1, -1)), (near_z, here - 2)]
    attend_earlier(
        place, segment_list, segments, query_segment, queries, blocks, top, total, mixed
    )


def attention_second(
    place, segment_list, segments, query_segment, queries, cross, far, far_cross, projection,
    top_in, total_in, mixed_in, sent, kept, top, total, mixed, attended,
):
    here, hd = place[0], place[1]
    odd = here % 2
    top[...] = top_in[...]
    total[...] = total_in[...]
    mixed[...] = mixed_in[...]
    blocks = [
        (cross, jnp.where(odd == 1, here - 3, here - 1)),
        (far, here - 4),
        (far_cross, jnp.where(odd == 1, -1, here - 3)),
    ]
    attend_earlier(
        place, segment_list, segments, query_segment, queries, blocks, top, total, mixed
    )
    for head in range(HEADS_HERE):
        attended[:, head * HD : (head + 1) * HD] = (
            mixed[head] / total[:, head : head + 1]
        ).astype(jnp.bfloat16)
    mate, across = hd ^ 1, hd ^ 2

    def rows_of(first, second):
        return jnp.concatenate(
            [
                attended[pl.ds(pl.multiple_of(quarter * ROWS, ROWS), ROWS), :]
                for quarter in (first, second)
            ],
            axis=0,
        )

    sent[...] = jnp.dot(
        rows_of(mate, mate ^ 2), projection[...], preferred_element_type=jnp.float32
    ).astype(jnp.bfloat16)
    kept[...] = jnp.dot(rows_of(hd, across), projection[...], preferred_element_type=jnp.float32)


def attention(
    place, segment_ids, query_segment, queries, own, near_x, near_z, cross, far, far_cross, out_proj
):
    segments = segment_ids.reshape(-1, BLOCK)
    state = (
        jax.ShapeDtypeStruct((BLOCK, HD), jnp.float32),
        jax.ShapeDtypeStruct((BLOCK, HD), jnp.float32),
        jax.ShapeDtypeStruct((HEADS_HERE, BLOCK, HD), jnp.float32),
    )
    smem, vmem = whole(pltpu.SMEM), whole()
    limit = pltpu.CompilerParams(vmem_limit_bytes=16 * 2**20)
    first = pl.pallas_call(
        attention_first,
        out_shape=state,
        in_specs=[smem, smem] + [vmem] * 6,
        out_specs=(vmem, vmem, vmem),
        compiler_params=limit,
        cost_estimate=pl.CostEstimate(flops=6 * 10**8, bytes_accessed=4 * 10**6, transcendentals=6 * 10**5),
    )(place, segment_ids, segments, query_segment, queries, own, near_x, near_z)
    return pl.pallas_call(
        attention_second,
        out_shape=(
            jax.ShapeDtypeStruct((2 * ROWS, out_proj.shape[1]), jnp.bfloat16),
            jax.ShapeDtypeStruct((2 * ROWS, out_proj.shape[1]), jnp.float32),
        ),
        in_specs=[smem, smem] + [vmem] * 10,
        out_specs=(vmem, vmem),
        scratch_shapes=[pltpu.VMEM(array.shape, jnp.float32) for array in state]
        + [pltpu.VMEM((BLOCK, HEADS_HERE * HD), jnp.bfloat16)],
        compiler_params=limit,
    )(
        place, segment_ids, segments, query_segment, queries, cross, far, far_cross, out_proj, *first
    )


CHUNK = 256
WIDE = 512
PIECE = 2 * ROWS
PIECES = 8
DEPTH = 3


def silu_times(gate_val, up_val):
    return (gate_val / (1.0 + jnp.exp(-gate_val)) * up_val).astype(jnp.bfloat16)


def routing_kernel(slot_row, weight_row, slot_column, pick, spread, slot_weight):
    slot_numbers = lax.broadcasted_iota(jnp.int32, (SLOTS, GROUP_ROWS), 0)
    slot_lanes = lax.broadcasted_iota(jnp.int32, (GROUP_ROWS, 2 * SLOTS), 1)
    for group in range(2):
        for expert in range(2):
            line = slice(2 * group + expert, 2 * group + expert + 1)
            held = slice(expert * SLOTS, (expert + 1) * SLOTS)
            hit = slot_row[line, :] == slot_numbers
            pick[group, held] = jnp.where(hit, 1.0, 0.0).astype(jnp.bfloat16)
            slot_weight[group, held] = jnp.sum(
                jnp.where(hit, weight_row[line, :], 0.0), axis=1, keepdims=True
            )
        first, second = [slot_column[:, 2 * group + e : 2 * group + e + 1] for e in range(2)]
        hit = (first == slot_lanes) | ((second >= 0) & (second + SLOTS == slot_lanes))
        spread[group] = jnp.where(hit, 1.0, 0.0).astype(jnp.bfloat16)


def routing_matrices(slot, weight):
    return pl.pallas_call(
        routing_kernel,
        out_shape=(
            jax.ShapeDtypeStruct((2, 2 * SLOTS, GROUP_ROWS), jnp.bfloat16),
            jax.ShapeDtypeStruct((2, GROUP_ROWS, 2 * SLOTS), jnp.bfloat16),
            jax.ShapeDtypeStruct((2, 2 * SLOTS, 1), jnp.float32),
        ),
        in_specs=[whole()] * 3,
        out_specs=(whole(),) * 3,
        compiler_params=pltpu.CompilerParams(vmem_limit_bytes=16 * 2**20),
    )(slot, weight, slot.T)


def experts_kernel(group, with_shared, *refs):
    place, pick, spread, slot_weight = refs[:4]
    pieces, refs = refs[4 : 4 + PIECES], refs[4 + PIECES :]
    gate, up, down = refs[:3]
    refs = refs[3:]
    if with_shared:
        shared, refs = refs[:3], refs[3:]
    targets, refs = refs[:PIECES], refs[PIECES:]
    rows, picked, hidden, gate_held, up_held, down_held, arrived, gate_up_arrived, down_arrived = refs[:9]
    width = rows.shape[1]
    chunks = [
        (expert, low, min(CHUNK, FF_E - low)) for expert in range(2) for low in range(0, FF_E, CHUNK)
    ]

    def gate_up_copies(number):
        expert, low, size = chunks[number]
        lanes, slot = pl.ds(expert * FF_E + low, size), number % DEPTH
        return [
            pltpu.make_async_copy(
                source.at[:, lanes], held.at[slot, :, pl.ds(0, size)], gate_up_arrived.at[slot, which]
            )
            for which, (source, held) in enumerate(((gate, gate_held), (up, up_held)))
        ]

    def down_copy(expert):
        return pltpu.make_async_copy(
            down.at[pl.ds(expert * FF_E, FF_E), :], down_held.at[expert], down_arrived.at[expert]
        )

    copies = [
        pltpu.make_async_copy(piece, rows.at[pl.ds(number * PIECE, PIECE), :], arrived.at[number])
        for number, piece in enumerate(pieces)
    ]
    for copy in copies:
        copy.start()
    for number in range(DEPTH):
        for copy in gate_up_copies(number):
            copy.start()
    down_copy(0).start()
    if with_shared:
        s_gate, s_up, s_down, s_arrived, s_rows, s_hidden = refs[9:]
        s_copies = [
            pltpu.make_async_copy(source, target, s_arrived.at[number])
            for number, (source, target) in enumerate(zip(shared, (s_gate, s_up, s_down)))
        ]

    for copy in copies:
        copy.wait()
    for low in range(0, width, WIDE):
        lanes = slice(low, low + WIDE)
        picked[:, lanes] = jnp.dot(
            pick[group], rows[:, lanes], preferred_element_type=jnp.float32
        ).astype(jnp.bfloat16)
    for number, (expert, low, size) in enumerate(chunks):
        held, slot = slice(expert * SLOTS, (expert + 1) * SLOTS), number % DEPTH
        for copy in gate_up_copies(number):
            copy.wait()
        gate_val = jnp.dot(picked[held], gate_held[slot, :, :size], preferred_element_type=jnp.float32)
        up_val = jnp.dot(picked[held], up_held[slot, :, :size], preferred_element_type=jnp.float32)
        hidden[:, low : low + size] = silu_times(gate_val, up_val)
        if number + DEPTH < len(chunks):
            for copy in gate_up_copies(number + DEPTH):
                copy.start()
        if number == len(chunks) // 2:
            down_copy(1).start()
        if with_shared and number == len(chunks) - DEPTH:
            for copy in s_copies:
                copy.start()
        if low + size == FF_E:
            down_copy(expert).wait()
            for start in range(0, width, WIDE):
                lanes = slice(start, start + WIDE)
                result = jnp.dot(
                    hidden[...], down_held[expert, :, lanes], preferred_element_type=jnp.float32
                )
                picked[held, lanes] = (result * slot_weight[group, held]).astype(jnp.bfloat16)

    if with_shared:
        upper = place[1] % 2 == 1
        s_rows[0:ROWS] = rows[0:ROWS]
        s_rows[ROWS : 2 * ROWS] = rows[PIECE : PIECE + ROWS]
        base = pl.multiple_of(jnp.where(upper, 2, 5) * PIECE, PIECE)
        s_rows[2 * ROWS : 3 * ROWS] = rows[pl.ds(base, ROWS), :]
        s_rows[3 * ROWS : 4 * ROWS] = rows[pl.ds(base + PIECE, ROWS), :]
        for copy in s_copies:
            copy.wait()
        turned = (((1,), (1,)), ((), ()))
        units = s_gate.shape[0]
        for low in range(0, units, CHUNK):
            size = min(CHUNK, units - low)
            gate_val, up_val = [
                lax.dot_general(
                    s_rows[...], weight[low : low + size, :], turned, preferred_element_type=jnp.float32
                )
                for weight in (s_gate, s_up)
            ]
            s_hidden[:, low : low + size] = silu_times(gate_val, up_val)

    for low in range(0, width, CHUNK):
        lanes = slice(low, low + CHUNK)
        value = jnp.dot(spread[group], picked[:, lanes], preferred_element_type=jnp.float32)
        if with_shared:
            s_result = jnp.dot(s_hidden[...], s_down[:, lanes], preferred_element_type=jnp.float32)
        for part, target in enumerate(targets):
            mine = value[part * PIECE : (part + 1) * PIECE]
            if with_shared and part in (0, 1, 2, 3, 5, 6):
                if part < 2:
                    term = s_result[part * ROWS : (part + 1) * ROWS]
                else:
                    start = (2 + (part - 2) % 3) * ROWS
                    here = upper if part < 4 else jnp.logical_not(upper)
                    term = jnp.where(here, s_result[start : start + ROWS], 0.0)
                target[:ROWS, lanes] = (mine[:ROWS] + term).astype(jnp.bfloat16)
                target[ROWS:, lanes] = mine[ROWS:].astype(jnp.bfloat16)
            else:
                target[:, lanes] = mine.astype(jnp.bfloat16)


def experts(place, group, matrices, pieces, weights, shared):
    width = pieces[0].shape[1]
    hbm, vmem = whole(pl.ANY), whole()
    scratch = [
        pltpu.VMEM((GROUP_ROWS, width), jnp.bfloat16),
        pltpu.VMEM((2 * SLOTS, width), jnp.bfloat16),
        pltpu.VMEM((SLOTS, FF_E), jnp.bfloat16),
        pltpu.VMEM((DEPTH, width, CHUNK), jnp.bfloat16),
        pltpu.VMEM((DEPTH, width, CHUNK), jnp.bfloat16),
        pltpu.VMEM((2, FF_E, width), jnp.bfloat16),
        pltpu.SemaphoreType.DMA((PIECES,)),
        pltpu.SemaphoreType.DMA((DEPTH, 2)),
        pltpu.SemaphoreType.DMA((2,)),
    ]
    operands = [place, *matrices, *pieces, *weights]
    if shared is not None:
        operands += list(shared)
        scratch += [pltpu.VMEM(array.shape, array.dtype) for array in shared]
        scratch += [
            pltpu.SemaphoreType.DMA((3,)),
            pltpu.VMEM((BLOCK, width), jnp.bfloat16),
            pltpu.VMEM((BLOCK, shared[2].shape[0]), jnp.bfloat16),
        ]
    in_specs = [whole(pltpu.SMEM)] + [vmem] * 3
    in_specs += [hbm] * (len(operands) - len(in_specs))
    return pl.pallas_call(
        lambda *refs: experts_kernel(group, shared is not None, *refs),
        out_shape=(jax.ShapeDtypeStruct((PIECE, width), jnp.bfloat16),) * PIECES,
        in_specs=in_specs,
        out_specs=(vmem,) * PIECES,
        scratch_shapes=scratch,
        compiler_params=pltpu.CompilerParams(vmem_limit_bytes=SCOPED[shared is not None] * 2**20),
        cost_estimate=pl.CostEstimate(
            flops=10**10, bytes_accessed=44 * 10**6, transcendentals=10**6
        ),
    )(*operands)


SCOPED = {True: 50, False: 40}


def gather_plane(rows):
    mate = send(rows, CORE_SWAP)
    near = send(rows, X_THEN_Y)
    near_mate = send(mate, X_THEN_Y)
    corner = send(near, Y_THEN_X)
    fetched = (near, near_mate, corner)
    return (rows, mate, *fetched, *[send(piece, CORE_SWAP) for piece in fetched])


def sum_plane(own, mate, near, near_mate, corner, mate_near, mate_near_mate, mate_corner):
    corner = added(corner, send(mate_corner, CORE_SWAP))
    from_corner = send(corner, Y_THEN_X)
    near_mate = added(near_mate, send(mate_near_mate, CORE_SWAP))
    from_near_mate = send(near_mate, X_THEN_Y)
    near = near.astype(jnp.float32) + send(mate_near, CORE_SWAP).astype(jnp.float32)
    from_near = send(added(near, from_corner), X_THEN_Y)
    return (
        own.astype(jnp.float32)
        + send(mate, CORE_SWAP).astype(jnp.float32)
        + send(from_near_mate, CORE_SWAP).astype(jnp.float32)
        + from_near.astype(jnp.float32)
    )


def routing_tables(expert_ids, route_weight, place):
    count = expert_ids.shape[1]
    packed = jnp.concatenate([expert_ids.T.astype(jnp.float32), route_weight.T], axis=0)
    pair = jnp.stack([packed, send(packed, X_SWAP)])
    steps = [pair]
    for _ in range(3):
        steps.append(send(steps[-1], Z_ON))
    slices = jnp.stack(steps).reshape(NZ, 2, 2 * count, 4, ROWS).transpose(0, 1, 3, 2, 4)
    slices = slices.reshape(-1, 2 * count, ROWS)
    order = lax.dynamic_index_in_dim(jnp.asarray(slice_order()), place[1], 0, keepdims=False)
    listed = slices[order.reshape(-1)].reshape(2, 16, 2 * count, ROWS)
    first_expert = 2 * (place[0] * 4 + place[1])
    local = (first_expert + lax.iota(jnp.int32, 2)).astype(jnp.float32)
    match = listed[:, None, :, :count] == local[None, :, None, None, None]
    hit = jnp.any(match, axis=3).reshape(2, 2, GROUP_ROWS)
    weight = jnp.sum(jnp.where(match, listed[:, None, :, count:], 0.0), axis=3)
    weight = weight.reshape(2, 2, GROUP_ROWS)
    ones = hit.astype(jnp.int32)
    slot = jnp.where(hit, jnp.cumsum(ones, axis=2) - 1, -1)
    return routing_matrices(slot.reshape(4, GROUP_ROWS), weight.reshape(4, GROUP_ROWS))


def block_pairs(target):
    pairs = []
    for z in range(NZ):
        for x in range(2):
            aim = target(z, x)
            if aim is not None and aim[0] < NZ:
                pairs.append((z * 2 + x, aim[0] * 2 + aim[1]))
    return pairs


def sliced_body(
    residual_in,
    queries,
    keys,
    values,
    segment_ids,
    out_proj,
    norm_gain,
    shared_gate,
    shared_up,
    shared_down,
    expert_gate,
    expert_up,
    expert_down,
    expert_ids,
    route_weight,
    block_table,
):
    tok_here = lax.axis_index("tok")
    hd_here = lax.axis_index("hd")
    place = jnp.stack([tok_here, hd_here]).astype(jnp.int32)
    page_count = BLOCK // PAGE
    own, kv_pages = write_pages(keys, values, block_table - tok_here * page_count)

    def move(array, target):
        return lax.ppermute(array, "tok", block_pairs(target))

    near_z = move(own, lambda z, x: (z + 1, x))
    own_later, ids_later, _ = lax.optimization_barrier((own, expert_ids, near_z))
    near_x = move(own_later, lambda z, x: (z, 1) if x == 0 else None)
    cross = move(near_z, lambda z, x: (z, 1 - x))
    far = move(near_z, lambda z, x: (z + 1, x))
    far_cross = move(near_z, lambda z, x: (z + 1, 0) if x == 1 else None)

    tables = routing_tables(ids_later, route_weight, place)
    query_segment = lax.dynamic_slice_in_dim(segment_ids, tok_here * BLOCK, BLOCK, 0)[:, None]
    sent, kept = attention(
        place, segment_ids, query_segment, queries, own, near_x, near_z, cross, far, far_cross, out_proj,
    )
    kept = kept + send(sent, CORE_SWAP).astype(jnp.float32)
    resid_rows = (
        lax.dynamic_slice_in_dim(residual_in, hd_here * ROWS, ROWS, 0).astype(jnp.float32)
        + kept[:ROWS]
        + send(kept[ROWS:].astype(jnp.bfloat16), Y_SWAP).astype(jnp.float32)
    )
    normed = rms_normed(resid_rows, norm_gain)

    steps = [normed]
    for _ in range(3):
        steps.append(send(steps[-1], Z_ON))
    weights = (expert_gate, expert_up, expert_down)
    shared = (shared_gate.T, shared_up.T, shared_down)
    sums = []
    for group in range(2):
        gathered = gather_plane(jnp.concatenate(steps[2 * group : 2 * group + 2], axis=0))
        terms = experts(place, group, tables, gathered, weights, shared if group == 0 else None)
        sums.append(sum_plane(*terms))
    returned = [
        send(part.astype(jnp.bfloat16), pairs).astype(jnp.float32)
        for part, pairs in ((sums[0][ROWS:], Z_BACK), (sums[1][:ROWS], Z_TWO), (sums[1][ROWS:], Z_ON))
    ]
    output = resid_rows + sums[0][:ROWS] + returned[0] + returned[1] + returned[2]
    return (output.astype(jnp.bfloat16), kv_pages)


def solution(mesh):
    placed = (
        P("tok", None),
        P("tok", "hd"),
        P("tok", "hd"),
        P("tok", "hd"),
        P(),
        P("hd", None),
        P(),
        P(None, "hd"),
        P(None, "hd"),
        P("hd", None),
        P(None, ("tok", "hd")),
        P(None, ("tok", "hd")),
        P(("tok", "hd"), None),
        P("tok", None),
        P("tok", None),
        P("tok"),
    )
    return jax.shard_map(
        sliced_body if dict(mesh.shape) == {"tok": 2 * NZ, "hd": 4} else general_body,
        mesh=mesh,
        in_specs=placed,
        out_specs=(P(("tok", "hd"), None), P("tok", None, "hd")),
        check_vma=False,
    )
```

profile of v0, /device:TPU:0, one launch (start us, length us, event | category | flops | bytes accessed | tf_op | source)
XLA Modules:
  0.0 253.9 jit_solution(13986897624213242174)
XLA Ops:
  4.1 5.7 %collective-permute-start = (bf16[256,1024]{1,0:T(8,128)(2,1)}, bf16[256,1024]{1,0:T(8,128)(2,1)}, u32[]{:S(2)}, u32[]{:S(2)}) collective-permute-start(bf16[256,1024]{1,0:T(8,128)(2,1)} %get-tuple-element.31.own), channel_id=1, source_target_pairs={{0,8},{4,12},{8,16},{12,20},{16,24},{20,28},{1,9},{5,13},{9,17},{1... | collective-permute-start | bytes 1572872 | tf_op jit(solution)/shard_map/ppermute | solution.py:695
  9.9 10.7 %collective-permute-done.near_z = bf16[256,1024]{1,0:T(8,128)(2,1)} collective-permute-done((bf16[256,1024]{1,0:T(8,128)(2,1)}, bf16[256,1024]{1,0:T(8,128)(2,1)}, u32[]{:S(2)}, u32[]{:S(2)}) %collective-permute-start) | collective-permute-done | bytes 524320 | tf_op jit(solution)/shard_map/ppermute | solution.py:695
  20.5 4.2 %collective-permute-start.4 = (bf16[256,1024]{1,0:T(8,128)(2,1)}, bf16[256,1024]{1,0:T(8,128)(2,1)}, u32[]{:S(2)}, u32[]{:S(2)}) collective-permute-start(bf16[256,1024]{1,0:T(8,128)(2,1)} %get-tuple-element.31.own), channel_id=1, source_target_pairs={{0,4},{8,12},{16,20},{24,28},{1,5},{9,13},{17,21},{25,29},{2,6},{1... | collective-permute-start | bytes 1572872 | tf_op jit(solution)/shard_map/ppermute | solution.py:695
  24.7 4.4 %collective-permute-start.2 = (bf16[256,1024]{1,0:T(8,128)(2,1)}, bf16[256,1024]{1,0:T(8,128)(2,1)S(1)}, u32[]{:S(2)}, u32[]{:S(2)}) collective-permute-start(bf16[256,1024]{1,0:T(8,128)(2,1)} %collective-permute-done.near_z), channel_id=1, source_target_pairs={{0,8},{4,12},{8,16},{12,20},{16,24},{20,28},{1,9},{5,13},{9,17},{1... | collective-permute-start | bytes 1572872 | tf_op jit(solution)/shard_map/ppermute | solution.py:695
  32.3 4.3 %collective-permute-done.4.near_x = bf16[256,1024]{1,0:T(8,128)(2,1)} collective-permute-done((bf16[256,1024]{1,0:T(8,128)(2,1)}, bf16[256,1024]{1,0:T(8,128)(2,1)}, u32[]{:S(2)}, u32[]{:S(2)}) %collective-permute-start.4) | collective-permute-done | bytes 524320 | tf_op jit(solution)/shard_map/ppermute | solution.py:695
  41.4 4.4 %collective-permute-done.1.cross = bf16[256,1024]{1,0:T(8,128)(2,1)S(1)} collective-permute-done((bf16[256,1024]{1,0:T(8,128)(2,1)}, bf16[256,1024]{1,0:T(8,128)(2,1)S(1)}, u32[]{:S(2)}, u32[]{:S(2)}) %collective-permute-start.1) | collective-permute-done | bytes 524320 | tf_op jit(solution)/shard_map/ppermute | solution.py:695
  50.4 2.7 %shard_map.178 = (bf16[128,2048]{1,0:T(8,128)(2,1)}, f32[128,2048]{1,0:T(8,128)S(1)}) custom-call(s32[2]{0:T(128)S(1)} %pad_add_fusion.place.refs_0_, s32[2048]{0:T(1024)S(1)} %copy-done.11, s32[8,256]{1,0:T(8,128)S(1)} %reshape.94.segments, s32[256,1]{1,0:T(8,128)S(1)} %copy.44.query_segment, bf16[256,512]{1,0:T(8,128)(2,1)S(1)} %copy-done.10, ...), custom_call_target="tpu_custom_call" | custom-call | tf_op jit(solution)/shard_map/pallas_call | solution.py:397
  57.0 5.1 %collective-permute-start.7 = (f32[12,256]{1,0:T(8,128)S(1)}, f32[12,256]{1,0:T(8,128)S(1)}, u32[]{:S(2)}, u32[]{:S(2)}) collective-permute-start(f32[12,256]{1,0:T(8,128)S(1)} %get-tuple-element.65), channel_id=1, source_target_pairs={{0,4},{1,5},{2,6},{3,7},{4,0},{5,1},{6,2},{7,3},{8,12},{9,13},{10,... | collective-permute-start | bytes 36872 | tf_op jit(solution)/shard_map/ppermute | solution.py:242
  65.9 9.5 %collective-permute-start.11 = (bf16[64,2048]{1,0:T(8,128)(2,1)S(1)}, bf16[64,2048]{1,0:T(8,128)(2,1)S(1)}, u32[]{:S(2)}, u32[]{:S(2)}) collective-permute-start(bf16[64,2048]{1,0:T(8,128)(2,1)S(1)} %multiply_convert_fusion), channel_id=1, source_target_pairs={{0,8},{1,9},{2,10},{3,11},{4,12},{5,13},{6,14},{7,15},{8,24},{9,25... | collective-permute-start | bytes 786440 | tf_op jit(solution)/shard_map/ppermute | solution.py:242
  75.4 2.6 %collective-permute-start.8 = (f32[2,12,256]{2,1,0:T(8,128)S(1)}, f32[2,12,256]{2,1,0:T(8,128)S(1)}, u32[]{:S(2)}, u32[]{:S(2)}) collective-permute-start(f32[2,12,256]{2,1,0:T(8,128)S(1)} %pad_maximum_fusion.1), channel_id=1, source_target_pairs={{0,8},{1,9},{2,10},{3,11},{4,12},{5,13},{6,14},{7,15},{8,24},{9,25... | collective-permute-start | bytes 73736 | tf_op jit(solution)/shard_map/ppermute | solution.py:242
  78.1 3.1 %collective-permute-done.8 = f32[2,12,256]{2,1,0:T(8,128)S(1)} collective-permute-done((f32[2,12,256]{2,1,0:T(8,128)S(1)}, f32[2,12,256]{2,1,0:T(8,128)S(1)}, u32[]{:S(2)}, u32[]{:S(2)}) %collective-permute-start.8) | collective-permute-done | bytes 24608 | tf_op jit(solution)/shard_map/ppermute | solution.py:242
  83.7 3.4 %collective-permute-start.28 = (bf16[64,2048]{1,0:T(8,128)(2,1)S(1)}, bf16[64,2048]{1,0:T(8,128)(2,1)S(1)}, u32[]{:S(2)}, u32[]{:S(2)}) collective-permute-start(bf16[64,2048]{1,0:T(8,128)(2,1)S(1)} %collective-permute-done.11), channel_id=1, source_target_pairs={{0,8},{1,9},{2,10},{3,11},{4,12},{5,13},{6,14},{7,15},{8,24},{9,25... | collective-permute-start | bytes 786440 | tf_op jit(solution)/shard_map/ppermute | solution.py:242
  94.4 5.6 %collective-permute-done.29 = bf16[64,2048]{1,0:T(8,128)(2,1)S(1)} collective-permute-done((bf16[64,2048]{1,0:T(8,128)(2,1)S(1)}, bf16[64,2048]{1,0:T(8,128)(2,1)S(1)}, u32[]{:S(2)}, u32[]{:S(2)}) %collective-permute-start.29) | collective-permute-done | bytes 262176 | tf_op jit(solution)/shard_map/ppermute | solution.py:242
  106.2 7.6 %collective-permute-done.31.refs_6_ = bf16[128,2048]{1,0:T(8,128)(2,1)S(1)} collective-permute-done((bf16[128,2048]{1,0:T(8,128)(2,1)S(1)}, bf16[128,2048]{1,0:T(8,128)(2,1)S(1)}, u32[]{:S(2)}, u32[]{:S(2)}) %collective-permute-start.31) | collective-permute-done | bytes 524320 | tf_op jit(solution)/shard_map/ppermute | solution.py:242
  114.3 10.8 %collective-permute-done.14.refs_7_ = bf16[128,2048]{1,0:T(8,128)(2,1)} collective-permute-done((bf16[128,2048]{1,0:T(8,128)(2,1)}, bf16[128,2048]{1,0:T(8,128)(2,1)}, u32[]{:S(2)}, u32[]{:S(2)}) %collective-permute-start.14) | collective-permute-done | bytes 524320 | tf_op jit(solution)/shard_map/ppermute | solution.py:242
  134.3 38.8 %shard_map.180 = (bf16[128,2048]{1,0:T(8,128)(2,1)S(1)}, bf16[128,2048]{1,0:T(8,128)(2,1)S(1)}, bf16[128,2048]{1,0:T(8,128)(2,1)S(1)}, bf16[128,2048]{1,0:T(8,12...) custom-call(s32[2]{0:T(128)S(1)} %pad_add_fusion.place.refs_0_, ...), custom_call_target="tpu_custom_call" | custom-call | flops 10000000000 | bytes 44000000 | tf_op jit(solution)/shard_map/pallas_call | solution.py:598
  174.1 18.4 %shard_map.181 = (bf16[128,2048]{1,0:T(8,128)(2,1)S(1)}, bf16[128,2048]{1,0:T(8,128)(2,1)S(1)}, bf16[128,2048]{1,0:T(8,128)(2,1)S(1)}, bf16[128,2048]{1,0:T(8,12...) custom-call(s32[2]{0:T(128)S(1)} %pad_add_fusion.place.refs_0_, ...), custom_call_target="tpu_custom_call" | custom-call | flops 10000000000 | bytes 44000000 | tf_op jit(solution)/shard_map/pallas_call | solution.py:598
  197.7 9.5 %collective-permute-done.21 = bf16[128,2048]{1,0:T(8,128)(2,1)S(1)} collective-permute-done((bf16[128,2048]{1,0:T(8,128)(2,1)S(1)}, bf16[128,2048]{1,0:T(8,128)(2,1)S(1)}, u32[]{:S(2)}, u32[]{:S(2)}) %collective-permute-start.21) | collective-permute-done | bytes 524320 | tf_op jit(solution)/shard_map/ppermute | solution.py:242
  209.5 9.1 %collective-permute-done.43 = bf16[128,2048]{1,0:T(8,128)(2,1)S(1)} collective-permute-done((bf16[128,2048]{1,0:T(8,128)(2,1)S(1)}, bf16[128,2048]{1,0:T(8,128)(2,1)S(1)}, u32[]{:S(2)}, u32[]{:S(2)}) %collective-permute-start.43) | collective-permute-done | bytes 524320 | tf_op jit(solution)/shard_map/ppermute | solution.py:242
  219.6 5.4 %collective-permute-done.26 = bf16[128,2048]{1,0:T(8,128)(2,1)S(1)} collective-permute-done((bf16[128,2048]{1,0:T(8,128)(2,1)S(1)}, bf16[128,2048]{1,0:T(8,128)(2,1)S(1)}, u32[]{:S(2)}, u32[]{:S(2)}) %collective-permute-start.26) | collective-permute-done | bytes 524320 | tf_op jit(solution)/shard_map/ppermute | solution.py:242
  226.2 4.4 %collective-permute-done.44 = bf16[128,2048]{1,0:T(8,128)(2,1)S(1)} collective-permute-done((bf16[128,2048]{1,0:T(8,128)(2,1)S(1)}, bf16[128,2048]{1,0:T(8,128)(2,1)S(1)}, u32[]{:S(2)}, u32[]{:S(2)}) %collective-permute-start.44) | collective-permute-done | bytes 524320 | tf_op jit(solution)/shard_map/ppermute | solution.py:242
  231.0 3.2 %collective-permute-start.45 = (bf16[64,2048]{1,0:T(8,128)(2,1)S(1)}, bf16[64,2048]{1,0:T(8,128)(2,1)S(1)}, u32[]{:S(2)}, u32[]{:S(2)}) collective-permute-start(bf16[64,2048]{1,0:T(8,128)(2,1)S(1)} %get-tuple-element.60), channel_id=1, source_target_pairs={{0,24},{1,25},{2,26},{3,27},{4,28},{5,29},{6,30},{7,31},{8,16},{9,... | collective-permute-start | bytes 786440 | tf_op jit(solution)/shard_map/ppermute | solution.py:242
  234.2 8.5 %collective-permute-done.45 = bf16[64,2048]{1,0:T(8,128)(2,1)S(1)} collective-permute-done((bf16[64,2048]{1,0:T(8,128)(2,1)S(1)}, bf16[64,2048]{1,0:T(8,128)(2,1)S(1)}, u32[]{:S(2)}, u32[]{:S(2)}) %collective-permute-start.45) | collective-permute-done | bytes 262176 | tf_op jit(solution)/shard_map/ppermute | solution.py:242
  242.6 10.3 %collective-permute-done.46 = bf16[64,2048]{1,0:T(8,128)(2,1)S(1)} collective-permute-done((bf16[64,2048]{1,0:T(8,128)(2,1)S(1)}, bf16[64,2048]{1,0:T(8,128)(2,1)S(1)}, u32[]{:S(2)}, u32[]{:S(2)}) %collective-permute-start.46) | collective-permute-done | bytes 262176 | tf_op jit(solution)/shard_map/ppermute | solution.py:242
  (176 shorter events, 61.1 us)
Async XLA Ops:
  4.1 16.4 %collective-permute-start = (bf16[256,1024]{1,0:T(8,128)(2,1)}, bf16[256,1024]{1,0:T(8,128)(2,1)}, u32[]{:S(2)}, u32[]{:S(2)}) collective-permute-start(bf16[256,1024]{1,0:T(8,128)(2,1)} %get-tuple-element.31.own), channel_id=1, source_target_pairs={{0,8},{4,12},{8,16},{12,20},{16,24},{20,28},{1,9},{5,13},{9,17},{1... | collective-permute-start | bytes 1572872 | tf_op jit(solution)/shard_map/ppermute | solution.py:695
  20.5 16.1 %collective-permute-start.4 = (bf16[256,1024]{1,0:T(8,128)(2,1)}, bf16[256,1024]{1,0:T(8,128)(2,1)}, u32[]{:S(2)}, u32[]{:S(2)}) collective-permute-start(bf16[256,1024]{1,0:T(8,128)(2,1)} %get-tuple-element.31.own), channel_id=1, source_target_pairs={{0,4},{8,12},{16,20},{24,28},{1,5},{9,13},{17,21},{25,29},{2,6},{1... | collective-permute-start | bytes 1572872 | tf_op jit(solution)/shard_map/ppermute | solution.py:695
  24.7 21.0 %collective-permute-start.1 = (bf16[256,1024]{1,0:T(8,128)(2,1)}, bf16[256,1024]{1,0:T(8,128)(2,1)S(1)}, u32[]{:S(2)}, u32[]{:S(2)}) collective-permute-start(bf16[256,1024]{1,0:T(8,128)(2,1)} %collective-permute-done.near_z), channel_id=1, source_target_pairs={{0,4},{4,0},{8,12},{12,8},{16,20},{20,16},{24,28},{28,24},{1,5},{5... | collective-permute-start | bytes 1572872 | tf_op jit(solution)/shard_map/ppermute | solution.py:695
  24.7 21.8 %collective-permute-start.2 = (bf16[256,1024]{1,0:T(8,128)(2,1)}, bf16[256,1024]{1,0:T(8,128)(2,1)S(1)}, u32[]{:S(2)}, u32[]{:S(2)}) collective-permute-start(bf16[256,1024]{1,0:T(8,128)(2,1)} %collective-permute-done.near_z), channel_id=1, source_target_pairs={{0,8},{4,12},{8,16},{12,20},{16,24},{20,28},{1,9},{5,13},{9,17},{1... | collective-permute-start | bytes 1572872 | tf_op jit(solution)/shard_map/ppermute | solution.py:695
  29.2 18.2 %collective-permute-start.3 = (bf16[256,1024]{1,0:T(8,128)(2,1)}, bf16[256,1024]{1,0:T(8,128)(2,1)}, u32[]{:S(2)}, u32[]{:S(2)}) collective-permute-start(bf16[256,1024]{1,0:T(8,128)(2,1)} %collective-permute-done.near_z), channel_id=1, source_target_pairs={{4,8},{12,16},{20,24},{5,9},{13,17},{21,25},{6,10},{14,18},{22,26}... | collective-permute-start | bytes 1572872 | tf_op jit(solution)/shard_map/ppermute | solution.py:695
  57.0 18.4 %collective-permute-start.7 = (f32[12,256]{1,0:T(8,128)S(1)}, f32[12,256]{1,0:T(8,128)S(1)}, u32[]{:S(2)}, u32[]{:S(2)}) collective-permute-start(f32[12,256]{1,0:T(8,128)S(1)} %get-tuple-element.65), channel_id=1, source_target_pairs={{0,4},{1,5},{2,6},{3,7},{4,0},{5,1},{6,2},{7,3},{8,12},{9,13},{10,... | collective-permute-start | bytes 36872 | tf_op jit(solution)/shard_map/ppermute | solution.py:242
  65.9 17.8 %collective-permute-start.11 = (bf16[64,2048]{1,0:T(8,128)(2,1)S(1)}, bf16[64,2048]{1,0:T(8,128)(2,1)S(1)}, u32[]{:S(2)}, u32[]{:S(2)}) collective-permute-start(bf16[64,2048]{1,0:T(8,128)(2,1)S(1)} %multiply_convert_fusion), channel_id=1, source_target_pairs={{0,8},{1,9},{2,10},{3,11},{4,12},{5,13},{6,14},{7,15},{8,24},{9,25... | collective-permute-start | bytes 786440 | tf_op jit(solution)/shard_map/ppermute | solution.py:242
  100.2 25.0 %collective-permute-start.14 = (bf16[128,2048]{1,0:T(8,128)(2,1)}, bf16[128,2048]{1,0:T(8,128)(2,1)}, u32[]{:S(2)}, u32[]{:S(2)}) collective-permute-start(bf16[128,2048]{1,0:T(8,128)(2,1)} %collective-permute-done.12.refs_5_), channel_id=1, source_target_pairs={{0,4},{1,3},{2,6},{3,1},{4,0},{5,7},{6,2},{7,5},{8,12},{9,11},{10,... | collective-permute-start | bytes 1572872 | tf_op jit(solution)/shard_map/ppermute | solution.py:242
  102.2 22.9 %collective-permute-start.15 = (bf16[128,2048]{1,0:T(8,128)(2,1)}, bf16[128,2048]{1,0:T(8,128)(2,1)}, u32[]{:S(2)}, u32[]{:S(2)}) collective-permute-start(bf16[128,2048]{1,0:T(8,128)(2,1)} %collective-permute-done.13.refs_6_), channel_id=1, source_target_pairs={{0,2},{1,5},{2,0},{3,7},{4,6},{5,1},{6,4},{7,3},{8,10},{9,13},{10,... | collective-permute-start | bytes 1572872 | tf_op jit(solution)/shard_map/ppermute | solution.py:242
  105.0 28.7 %collective-permute-start.16 = (bf16[128,2048]{1,0:T(8,128)(2,1)}, bf16[128,2048]{1,0:T(8,128)(2,1)}, u32[]{:S(2)}, u32[]{:S(2)}) collective-permute-start(bf16[128,2048]{1,0:T(8,128)(2,1)} %collective-permute-done.13.refs_6_), channel_id=1, source_target_pairs={{0,1},{1,0},{2,3},{3,2},{4,5},{5,4},{6,7},{7,6},{8,9},{9,8},{10,11... | collective-permute-start | bytes 1572872 | tf_op jit(solution)/shard_map/ppermute | solution.py:242
  105.1 28.6 %collective-permute-start.32 = (bf16[128,2048]{1,0:T(8,128)(2,1)S(1)}, bf16[128,2048]{1,0:T(8,128)(2,1)S(1)}, u32[]{:S(2)}, u32[]{:S(2)}) collective-permute-start(bf16[128,2048]{1,0:T(8,128)(2,1)S(1)} %collective-permute-done.30.refs_5_), channel_id=1, source_target_pairs={{0,4},{1,3},{2,6},{3,1},{4,0},{5,7},{6,2},{7,5},{8,12},{9,11},{10,... | collective-permute-start | bytes 1572872 | tf_op jit(solution)/shard_map/ppermute | solution.py:242
  113.8 20.4 %collective-permute-start.33 = (bf16[128,2048]{1,0:T(8,128)(2,1)S(1)}, bf16[128,2048]{1,0:T(8,128)(2,1)S(1)}, u32[]{:S(2)}, u32[]{:S(2)}) collective-permute-start(bf16[128,2048]{1,0:T(8,128)(2,1)S(1)} %collective-permute-done.31.refs_6_), channel_id=1, source_target_pairs={{0,2},{1,5},{2,0},{3,7},{4,6},{5,1},{6,4},{7,3},{8,10},{9,13},{10,... | collective-permute-start | bytes 1572872 | tf_op jit(solution)/shard_map/ppermute | solution.py:242
  133.7 40.0 %collective-permute-start.34 = (bf16[128,2048]{1,0:T(8,128)(2,1)S(1)}, bf16[128,2048]{1,0:T(8,128)(2,1)S(1)}, u32[]{:S(2)}, u32[]{:S(2)}) collective-permute-start(bf16[128,2048]{1,0:T(8,128)(2,1)S(1)} %collective-permute-done.31.refs_6_), channel_id=1, source_target_pairs={{0,1},{1,0},{2,3},{3,2},{4,5},{5,4},{6,7},{7,6},{8,9},{9,8},{10,11... | collective-permute-start | bytes 1572872 | tf_op jit(solution)/shard_map/ppermute | solution.py:242
  133.7 40.4 %collective-permute-start.35 = (bf16[128,2048]{1,0:T(8,128)(2,1)S(1)}, bf16[128,2048]{1,0:T(8,128)(2,1)S(1)}, u32[]{:S(2)}, u32[]{:S(2)}) collective-permute-start(bf16[128,2048]{1,0:T(8,128)(2,1)S(1)} %collective-permute-done.32.refs_7_), channel_id=1, source_target_pairs={{0,1},{1,0},{2,3},{3,2},{4,5},{5,4},{6,7},{7,6},{8,9},{9,8},{10,11... | collective-permute-start | bytes 1572872 | tf_op jit(solution)/shard_map/ppermute | solution.py:242
  134.2 39.9 %collective-permute-start.36 = (bf16[128,2048]{1,0:T(8,128)(2,1)S(1)}, bf16[128,2048]{1,0:T(8,128)(2,1)S(1)}, u32[]{:S(2)}, u32[]{:S(2)}) collective-permute-start(bf16[128,2048]{1,0:T(8,128)(2,1)S(1)} %collective-permute-done.33.refs_8_), channel_id=1, source_target_pairs={{0,1},{1,0},{2,3},{3,2},{4,5},{5,4},{6,7},{7,6},{8,9},{9,8},{10,11... | collective-permute-start | bytes 1572872 | tf_op jit(solution)/shard_map/ppermute | solution.py:242
  173.1 20.0 %collective-permute-start.20 = (bf16[128,2048]{1,0:T(8,128)(2,1)S(1)}, bf16[128,2048]{1,0:T(8,128)(2,1)S(1)}, u32[]{:S(2)}, u32[]{:S(2)}) collective-permute-start(bf16[128,2048]{1,0:T(8,128)(2,1)S(1)} %get-tuple-element.44), channel_id=1, source_target_pairs={{0,1},{1,0},{2,3},{3,2},{4,5},{5,4},{6,7},{7,6},{8,9},{9,8},{10,11... | collective-permute-start | bytes 1572872 | tf_op jit(solution)/shard_map/ppermute | solution.py:242
  173.6 19.7 %collective-permute-start.24 = (bf16[128,2048]{1,0:T(8,128)(2,1)}, bf16[128,2048]{1,0:T(8,128)(2,1)S(1)}, u32[]{:S(2)}, u32[]{:S(2)}) collective-permute-start(bf16[128,2048]{1,0:T(8,128)(2,1)} %get-tuple-element.48), channel_id=1, source_target_pairs={{0,1},{1,0},{2,3},{3,2},{4,5},{5,4},{6,7},{7,6},{8,9},{9,8},{10,11... | collective-permute-start | bytes 1572872 | tf_op jit(solution)/shard_map/ppermute | solution.py:242
  173.7 23.9 %collective-permute-start.23 = (bf16[128,2048]{1,0:T(8,128)(2,1)S(1)}, bf16[128,2048]{1,0:T(8,128)(2,1)S(1)}, u32[]{:S(2)}, u32[]{:S(2)}) collective-permute-start(bf16[128,2048]{1,0:T(8,128)(2,1)S(1)} %get-tuple-element.46), channel_id=1, source_target_pairs={{0,1},{1,0},{2,3},{3,2},{4,5},{5,4},{6,7},{7,6},{8,9},{9,8},{10,11... | collective-permute-start | bytes 1572872 | tf_op jit(solution)/shard_map/ppermute | solution.py:242
  193.1 15.5 %collective-permute-start.41 = (bf16[128,2048]{1,0:T(8,128)(2,1)S(1)}, bf16[128,2048]{1,0:T(8,128)(2,1)S(1)}, u32[]{:S(2)}, u32[]{:S(2)}) collective-permute-start(bf16[128,2048]{1,0:T(8,128)(2,1)S(1)} %get-tuple-element.54), channel_id=1, source_target_pairs={{0,1},{1,0},{2,3},{3,2},{4,5},{5,4},{6,7},{7,6},{8,9},{9,8},{10,11... | collective-permute-start | bytes 1572872 | tf_op jit(solution)/shard_map/ppermute | solution.py:242
  193.3 13.8 %collective-permute-start.21 = (bf16[128,2048]{1,0:T(8,128)(2,1)S(1)}, bf16[128,2048]{1,0:T(8,128)(2,1)S(1)}, u32[]{:S(2)}, u32[]{:S(2)}) collective-permute-start(bf16[128,2048]{1,0:T(8,128)(2,1)S(1)} %add_convert_fusion.6), channel_id=1, source_target_pairs={{0,4},{1,3},{2,6},{3,1},{4,0},{5,7},{6,2},{7,5},{8,12},{9,11},{10,... | collective-permute-start | bytes 1572872 | tf_op jit(solution)/shard_map/ppermute | solution.py:242
  195.9 22.7 %collective-permute-start.43 = (bf16[128,2048]{1,0:T(8,128)(2,1)S(1)}, bf16[128,2048]{1,0:T(8,128)(2,1)S(1)}, u32[]{:S(2)}, u32[]{:S(2)}) collective-permute-start(bf16[128,2048]{1,0:T(8,128)(2,1)S(1)} %add_convert_fusion.2), channel_id=1, source_target_pairs={{0,2},{1,5},{2,0},{3,7},{4,6},{5,1},{6,4},{7,3},{8,10},{9,13},{10,... | collective-permute-start | bytes 1572872 | tf_op jit(solution)/shard_map/ppermute | solution.py:242
  197.6 21.2 %collective-permute-start.19 = (bf16[128,2048]{1,0:T(8,128)(2,1)S(1)}, bf16[128,2048]{1,0:T(8,128)(2,1)S(1)}, u32[]{:S(2)}, u32[]{:S(2)}) collective-permute-start(bf16[128,2048]{1,0:T(8,128)(2,1)S(1)} %get-tuple-element.42), channel_id=1, source_target_pairs={{0,1},{1,0},{2,3},{3,2},{4,5},{5,4},{6,7},{7,6},{8,9},{9,8},{10,11... | collective-permute-start | bytes 1572872 | tf_op jit(solution)/shard_map/ppermute | solution.py:242
  208.5 16.5 %collective-permute-start.26 = (bf16[128,2048]{1,0:T(8,128)(2,1)S(1)}, bf16[128,2048]{1,0:T(8,128)(2,1)S(1)}, u32[]{:S(2)}, u32[]{:S(2)}) collective-permute-start(bf16[128,2048]{1,0:T(8,128)(2,1)S(1)} %add_convert_fusion.4), channel_id=1, source_target_pairs={{0,4},{1,3},{2,6},{3,1},{4,0},{5,7},{6,2},{7,5},{8,12},{9,11},{10,... | collective-permute-start | bytes 1572872 | tf_op jit(solution)/shard_map/ppermute | solution.py:242
  234.2 18.7 %collective-permute-start.46 = (bf16[64,2048]{1,0:T(8,128)(2,1)S(1)}, bf16[64,2048]{1,0:T(8,128)(2,1)S(1)}, u32[]{:S(2)}, u32[]{:S(2)}) collective-permute-start(bf16[64,2048]{1,0:T(8,128)(2,1)S(1)} %get-tuple-element.61), channel_id=1, source_target_pairs={{0,8},{1,9},{2,10},{3,11},{4,12},{5,13},{6,14},{7,15},{8,24},{9,25... | collective-permute-start | bytes 786440 | tf_op jit(solution)/shard_map/ppermute | solution.py:242
  (42 other events, 425.1 us)
where the time goes:
time: 259 us; the launch traced here: 254 us
  waiting for transfers between devices  101 us (39%)
  Pallas kernels  66.2 us (26%)
  starting transfers between devices  60.2 us (23%)
  local copies, waits for them, and re-layouts  16.2 us (6%)
  other arithmetic  8.49 us (3%)
    ppermute x42, waiting for transfers between devices, send(): return lax.ppermute(array, BOTH, pairs)  82.1 us
    pallas_call x2, Pallas kernels, experts(): pl.pallas_call(lambda *refs: experts_kernel(group, shared is not None, *r...  57.1 us
    ppermute x42, starting transfers between devices, send(): return lax.ppermute(array, BOTH, pairs)  44.4 us
    ppermute x5, waiting for transfers between devices, move(): return lax.ppermute(array, 'tok', block_pairs(target))  19.3 us
    ppermute x5, starting transfers between devices, move(): return lax.ppermute(array, 'tok', block_pairs(target))  15.8 us
    unnamed x40, local copies, waits for them, and re-layouts  10.4 us
  transfers between devices with their start and end apart: 47, of which 19 were waited for; matrix products, arithmetic and copies ran while one was open for 5% of the time, Pallas kernels for 24%

commit v1 on v0

--- a/solution.py
+++ b/solution.py
@@ -250,17 +250,17 @@
     return pl.BlockSpec(memory_space=space)
 
 
-def pages_kernel(table, keys, values, joined, pages):
+def pages_kernel(table, place, keys, values, joined, pages):
     heads = keys.shape[1] // HD
     for head in range(heads):
         lanes = slice(head * HD, (head + 1) * HD)
         joined[:, 2 * head * HD : (2 * head + 1) * HD] = keys[:, lanes]
         joined[:, (2 * head + 1) * HD : (2 * head + 2) * HD] = values[:, lanes]
     for page in range(keys.shape[0] // PAGE):
-        pages[table[page]] = joined[page * PAGE : (page + 1) * PAGE, :]
-
-
-def write_pages(keys, values, local_pages):
+        pages[table[page] - place[0] * (keys.shape[0] // PAGE)] = joined[page * PAGE : (page + 1) * PAGE, :]
+
+
+def write_pages(keys, values, block_table, place):
     rows, width = keys.shape
     return pl.pallas_call(
         pages_kernel,
@@ -268,24 +268,33 @@
             jax.ShapeDtypeStruct((rows, 2 * width), keys.dtype),
             jax.ShapeDtypeStruct((rows // PAGE, PAGE, 2 * width), keys.dtype),
         ),
-        in_specs=[whole(pltpu.SMEM), whole(), whole()],
+        in_specs=[whole(pltpu.SMEM), whole(pltpu.SMEM), whole(), whole()],
         out_specs=(whole(), whole()),
-    )(local_pages, keys, values)
+    )(block_table, place, keys, values)
 
 
 HEADS_HERE = 4
 
 
-def attend_block(segments, query_segment, queries, block, source, diagonal, top, total, mixed):
-    allowed = segments[pl.ds(source, 1), :] == query_segment[...]
-    if diagonal:
-        rows = lax.broadcasted_iota(jnp.int32, (BLOCK, BLOCK), 0)
-        columns = lax.broadcasted_iota(jnp.int32, (BLOCK, BLOCK), 1)
-        allowed = allowed & (columns <= rows)
+def attend(place, segments, query_segment, queries, blocks):
+    offsets = lax.broadcasted_iota(jnp.int32, (1, BLOCK), 1)
+    key_segment, key_place = [], []
+    for _, source in blocks:
+        line = segments[pl.ds(jnp.maximum(source, 0), 1), :]
+        key_segment.append(jnp.where(source >= 0, line, -1))
+        key_place.append(source * BLOCK + offsets)
+    query_place = place[0] * BLOCK + lax.broadcasted_iota(jnp.int32, (BLOCK, 1), 0)
+    allowed = (jnp.concatenate(key_segment, axis=1) == query_segment[...]) & (
+        jnp.concatenate(key_place, axis=1) <= query_place
+    )
+    results = []
     for head in range(HEADS_HERE):
-        lane = slice(head, head + 1)
-        key = block[:, 2 * head * HD : (2 * head + 1) * HD]
-        value = block[:, (2 * head + 1) * HD : (2 * head + 2) * HD]
+        key, value = [
+            jnp.concatenate(
+                [block[:, (2 * head + part) * HD : (2 * head + part + 1) * HD] for block, _ in blocks], axis=0
+            )
+            for part in range(2)
+        ]
         scores = lax.dot_general(
             queries[:, head * HD : (head + 1) * HD],
             key,
@@ -294,69 +303,43 @@
         ) * (1.0 / math.sqrt(HD))
         scores = jnp.where(allowed, scores, MASKED_SCORE)
         largest = jnp.max(scores, axis=1, keepdims=True)
-        if not diagonal:
-            before = top[:, lane]
-            largest = jnp.maximum(largest, before)
-        exp_scores = jnp.exp(scores - largest)
-        update = jnp.dot(exp_scores.astype(jnp.bfloat16), value, preferred_element_type=jnp.float32)
-        added_up = jnp.sum(exp_scores, axis=1, keepdims=True)
-        if not diagonal:
-            shrink = jnp.exp(before - largest)
-            added_up += total[:, lane] * shrink
-            update += mixed[head] * shrink
-        top[:, lane] = largest
-        total[:, lane] = added_up
-        mixed[head] = update
-
-
-def attend_earlier(place, segment_list, segments, query_segment, queries, blocks, top, total, mixed):
-    for block, source in blocks:
-        safe = jnp.maximum(source, 0)
-        live = (source >= 0) & (
-            segment_list[safe * BLOCK + BLOCK - 1] == segment_list[place[0] * BLOCK]
-        )
-
-        @pl.when(live)
-        def _():
-            attend_block(
-                segments, query_segment, queries, block, safe, False, top, total, mixed
-            )
+        exp_scores = jnp.where(allowed, jnp.exp(scores - largest), 0.0)
+        mixed = jnp.dot(exp_scores.astype(jnp.bfloat16), value, preferred_element_type=jnp.float32)
+        results.append((largest, jnp.sum(exp_scores, axis=1, keepdims=True), mixed))
+    return results
 
 
 def attention_first(
-    place, segment_list, segments, query_segment, queries, own, near_x, near_z, top, total, mixed
+    place, segments, query_segment, queries, own, near_x, near_z, after, top, total, mixed
 ):
     here = place[0]
-    top[...] = jnp.zeros_like(top)
-    total[...] = jnp.ones_like(total)
-    attend_block(segments, query_segment, queries, own, here, True, top, total, mixed)
-    odd = here % 2
-    blocks = [(near_x, jnp.where(odd == 1, here - 1, -1)), (near_z, here - 2)]
-    attend_earlier(
-        place, segment_list, segments, query_segment, queries, blocks, top, total, mixed
-    )
+    blocks = [(own, here), (near_x, jnp.where(here % 2 == 1, here - 1, -1)), (near_z, here - 2)]
+    results = attend(place, segments, query_segment, queries, blocks)
+    top[...] = jnp.concatenate([result[0] for result in results], axis=1)
+    total[...] = jnp.concatenate([result[1] for result in results], axis=1)
+    for head in range(HEADS_HERE):
+        mixed[head] = results[head][2]
 
 
 def attention_second(
-    place, segment_list, segments, query_segment, queries, cross, far, far_cross, projection,
-    top_in, total_in, mixed_in, sent, kept, top, total, mixed, attended,
+    place, segments, query_segment, queries, cross, far, far_cross, projection,
+    top, total, mixed, after, sent, kept, attended,
 ):
     here, hd = place[0], place[1]
     odd = here % 2
-    top[...] = top_in[...]
-    total[...] = total_in[...]
-    mixed[...] = mixed_in[...]
     blocks = [
         (cross, jnp.where(odd == 1, here - 3, here - 1)),
         (far, here - 4),
         (far_cross, jnp.where(odd == 1, -1, here - 3)),
     ]
-    attend_earlier(
-        place, segment_list, segments, query_segment, queries, blocks, top, total, mixed
-    )
-    for head in range(HEADS_HERE):
+    results = attend(place, segments, query_segment, queries, blocks)
+    for head, (largest, added_up, update) in enumerate(results):
+        before = top[:, head : head + 1]
+        both = jnp.maximum(before, largest)
+        old, new = jnp.exp(before - both), jnp.exp(largest - both)
+        denom = total[:, head : head + 1] * old + added_up * new
         attended[:, head * HD : (head + 1) * HD] = (
-            mixed[head] / total[:, head : head + 1]
+            (mixed[head] * old + update * new) / denom
         ).astype(jnp.bfloat16)
     mate, across = hd ^ 1, hd ^ 2
 
@@ -376,38 +359,65 @@
 
 
 def attention(
-    place, segment_ids, query_segment, queries, own, near_x, near_z, cross, far, far_cross, out_proj
+    place, segment_ids, query_segment, queries, own, near_x, near_z, cross, far, far_cross, out_proj, after
 ):
     segments = segment_ids.reshape(-1, BLOCK)
     state = (
-        jax.ShapeDtypeStruct((BLOCK, HD), jnp.float32),
-        jax.ShapeDtypeStruct((BLOCK, HD), jnp.float32),
+        jax.ShapeDtypeStruct((BLOCK, HEADS_HERE), jnp.float32),
+        jax.ShapeDtypeStruct((BLOCK, HEADS_HERE), jnp.float32),
         jax.ShapeDtypeStruct((HEADS_HERE, BLOCK, HD), jnp.float32),
     )
-    smem, vmem = whole(pltpu.SMEM), whole()
-    limit = pltpu.CompilerParams(vmem_limit_bytes=16 * 2**20)
+    smem, vmem, anywhere = whole(pltpu.SMEM), whole(), whole(pl.ANY)
+    limit = pltpu.CompilerParams(vmem_limit_bytes=24 * 2**20)
     first = pl.pallas_call(
         attention_first,
         out_shape=state,
-        in_specs=[smem, smem] + [vmem] * 6,
+        in_specs=[smem] + [vmem] * 6 + [anywhere],
         out_specs=(vmem, vmem, vmem),
         compiler_params=limit,
-        cost_estimate=pl.CostEstimate(flops=6 * 10**8, bytes_accessed=4 * 10**6, transcendentals=6 * 10**5),
-    )(place, segment_ids, segments, query_segment, queries, own, near_x, near_z)
+        cost_estimate=pl.CostEstimate(flops=8 * 10**8, bytes_accessed=4 * 10**6, transcendentals=8 * 10**5),
+    )(place, segments, query_segment, queries, own, near_x, near_z, after[0])
     return pl.pallas_call(
         attention_second,
         out_shape=(
             jax.ShapeDtypeStruct((2 * ROWS, out_proj.shape[1]), jnp.bfloat16),
             jax.ShapeDtypeStruct((2 * ROWS, out_proj.shape[1]), jnp.float32),
         ),
-        in_specs=[smem, smem] + [vmem] * 10,
+        in_specs=[smem] + [vmem] * 10 + [anywhere],
         out_specs=(vmem, vmem),
-        scratch_shapes=[pltpu.VMEM(array.shape, jnp.float32) for array in state]
-        + [pltpu.VMEM((BLOCK, HEADS_HERE * HD), jnp.bfloat16)],
+        scratch_shapes=[pltpu.VMEM((BLOCK, HEADS_HERE * HD), jnp.bfloat16)],
         compiler_params=limit,
+        cost_estimate=pl.CostEstimate(flops=10**9, bytes_accessed=6 * 10**6, transcendentals=8 * 10**5),
     )(
-        place, segment_ids, segments, query_segment, queries, cross, far, far_cross, out_proj, *first
-    )
+        place, segments, query_segment, queries, cross, far, far_cross, out_proj, *first, after[1]
+    )
+
+
+def touch(arrays, after):
+    count = len(arrays)
+
+    def kernel(*refs):
+        sources, token, strips, arrived = refs[:count], refs[count + 1], refs[count + 2 : -1], refs[-1]
+        copies = [
+            pltpu.make_async_copy(source.at[:, pl.ds(0, HD)], strip, arrived.at[number])
+            for number, (source, strip) in enumerate(zip(sources, strips))
+        ]
+        for copy in copies:
+            copy.start()
+        token[...] = jnp.zeros_like(token)
+        for copy in copies:
+            copy.wait()
+
+    return pl.pallas_call(
+        kernel,
+        out_shape=jax.ShapeDtypeStruct((8, HD), jnp.float32),
+        in_specs=[whole(pltpu.HBM)] * count + [whole(pl.ANY)],
+        out_specs=whole(),
+        scratch_shapes=[pltpu.VMEM((array.shape[0], HD), array.dtype) for array in arrays]
+        + [pltpu.SemaphoreType.DMA((count,))],
+        compiler_params=pltpu.CompilerParams(vmem_limit_bytes=58 * 2**20),
+        cost_estimate=pl.CostEstimate(flops=0, bytes_accessed=3 * 10**6, transcendentals=0),
+    )(*arrays, after)
 
 
 CHUNK = 256
@@ -639,9 +649,7 @@
     count = expert_ids.shape[1]
     packed = jnp.concatenate([expert_ids.T.astype(jnp.float32), route_weight.T], axis=0)
     pair = jnp.stack([packed, send(packed, X_SWAP)])
-    steps = [pair]
-    for _ in range(3):
-        steps.append(send(steps[-1], Z_ON))
+    steps = [pair, send(pair, Z_ON), send(pair, Z_TWO), send(pair, Z_BACK)]
     slices = jnp.stack(steps).reshape(NZ, 2, 2 * count, 4, ROWS).transpose(0, 1, 3, 2, 4)
     slices = slices.reshape(-1, 2 * count, ROWS)
     order = lax.dynamic_index_in_dim(jnp.asarray(slice_order()), place[1], 0, keepdims=False)
@@ -688,23 +696,27 @@
     tok_here = lax.axis_index("tok")
     hd_here = lax.axis_index("hd")
     place = jnp.stack([tok_here, hd_here]).astype(jnp.int32)
-    page_count = BLOCK // PAGE
-    own, kv_pages = write_pages(keys, values, block_table - tok_here * page_count)
+    own, kv_pages = write_pages(keys, values, block_table, place)
 
     def move(array, target):
         return lax.ppermute(array, "tok", block_pairs(target))
 
     near_z = move(own, lambda z, x: (z + 1, x))
-    own_later, ids_later, _ = lax.optimization_barrier((own, expert_ids, near_z))
+    own_later, _ = lax.optimization_barrier((own, near_z))
     near_x = move(own_later, lambda z, x: (z, 1) if x == 0 else None)
+    weights = (expert_gate, expert_up, expert_down)
+    shared = (shared_gate.T, shared_up.T, shared_down)
+    touched = touch((*weights, *shared), own)
+    near_z, touched = lax.optimization_barrier((near_z, touched))
     cross = move(near_z, lambda z, x: (z, 1 - x))
     far = move(near_z, lambda z, x: (z + 1, x))
     far_cross = move(near_z, lambda z, x: (z + 1, 0) if x == 1 else None)
 
-    tables = routing_tables(ids_later, route_weight, place)
+    tables = routing_tables(expert_ids, route_weight, place)
     query_segment = lax.dynamic_slice_in_dim(segment_ids, tok_here * BLOCK, BLOCK, 0)[:, None]
     sent, kept = attention(
         place, segment_ids, query_segment, queries, own, near_x, near_z, cross, far, far_cross, out_proj,
+        (touched, touched),
     )
     kept = kept + send(sent, CORE_SWAP).astype(jnp.float32)
     resid_rows = (
@@ -717,8 +729,6 @@
     steps = [normed]
     for _ in range(3):
         steps.append(send(steps[-1], Z_ON))
-    weights = (expert_gate, expert_up, expert_down)
-    shared = (shared_gate.T, shared_up.T, shared_down)
     sums = []
     for group in range(2):
         gathered = gather_plane(jnp.concatenate(steps[2 * group : 2 * group + 2], axis=0))

time: 259 us -> 250 us (0.965); the launches traced: 254 us -> 248 us
  waiting for transfers between devices: 101 us -> 92.5 us
  local copies, waits for them, and re-layouts: 16.2 us -> 8.23 us
  starting transfers between devices: 60.2 us -> 67.9 us
  Pallas kernels: 66.2 us -> 70.4 us
    ppermute x42, waiting for transfers between devices: 82.1 us -> 74.3 us  [send(): return lax.ppermute(array, BOTH, pairs)]
    ppermute x42, starting transfers between devices: 44.4 us -> 51.2 us  [send(): return lax.ppermute(array, BOTH, pairs)]
    unnamed x40 -> x34, local copies, waits for them, and re-layouts: 10.4 us -> 3.85 us
    pallas_call x1 -> x2, Pallas kernels: 2.11 us -> 5.7 us  [the longest x1 3.36 us: attention(): pl.pallas_call(attention_first, out_shape=state, in_specs=[smem] + [vmem]...]
    pallas_call x1, Pallas kernels: 2.72 us -> 5.48 us  [attention(): pl.pallas_call(attention_second, out_shape=(jax.ShapeDtypeStruct((2 * ROW...]
  transfers between devices with their start and end apart: 47 -> 47, of which waited for: 19 -> 15; matrix products, arithmetic and copies ran while one was open for 5% -> 4% of each run, Pallas kernels for 24% -> 25%
where the time goes in v1:
time: 250 us; the launch traced here: 248 us
  waiting for transfers between devices  92.5 us (37%)
  Pallas kernels  70.4 us (28%)
  starting transfers between devices  67.9 us (27%)
  local copies, waits for them, and re-layouts  8.23 us (3%)
  other arithmetic  7.67 us (3%)
    ppermute x42, waiting for transfers between devices, send(): return lax.ppermute(array, BOTH, pairs)  74.3 us
    pallas_call x2, Pallas kernels, experts(): pl.pallas_call(lambda *refs: experts_kernel(group, shared is not None, *r...  55 us
    ppermute x42, starting transfers between devices, send(): return lax.ppermute(array, BOTH, pairs)  51.2 us
    ppermute x5, waiting for transfers between devices, move(): return lax.ppermute(array, 'tok', block_pairs(target))  18.2 us
    ppermute x5, starting transfers between devices, move(): return lax.ppermute(array, 'tok', block_pairs(target))  16.8 us
    pallas_call x1, Pallas kernels, attention(): pl.pallas_call(attention_second, out_shape=(jax.ShapeDtypeStruct((2 * ROW...  5.48 us
  transfers between devices with their start and end apart: 47, of which 15 were waited for; matrix products, arithmetic and copies ran while one was open for 4% of the time, Pallas kernels for 25%

profile of v1, /device:TPU:0, one launch (start us, length us, event | category | flops | bytes accessed | tf_op | source)
XLA Modules:
  0.0 248.1 jit_solution(10382302677454803884)
XLA Ops:
  3.4 5.7 %collective-permute-start = (bf16[256,1024]{1,0:T(8,128)(2,1)}, bf16[256,1024]{1,0:T(8,128)(2,1)}, u32[]{:S(2)}, u32[]{:S(2)}) collective-permute-start(bf16[256,1024]{1,0:T(8,128)(2,1)} %get-tuple-element.33.refs_6_.own), channel_id=1, source_target_pairs={{0,8},{4,12},{8,16},{12,20},{16,24},{20,28},{1,9},{5,13},{9,17},{1... | collective-permute-start | bytes 1572872 | tf_op jit(solution)/shard_map/ppermute | solution.py:702
  9.1 10.7 %collective-permute-done.near_z = bf16[256,1024]{1,0:T(8,128)(2,1)} collective-permute-done((bf16[256,1024]{1,0:T(8,128)(2,1)}, bf16[256,1024]{1,0:T(8,128)(2,1)}, u32[]{:S(2)}, u32[]{:S(2)}) %collective-permute-start) | collective-permute-done | bytes 524320 | tf_op jit(solution)/shard_map/ppermute | solution.py:702
  19.8 4.2 %collective-permute-start.4 = (bf16[256,1024]{1,0:T(8,128)(2,1)}, bf16[256,1024]{1,0:T(8,128)(2,1)}, u32[]{:S(2)}, u32[]{:S(2)}) collective-permute-start(bf16[256,1024]{1,0:T(8,128)(2,1)} %get-tuple-element.33.refs_6_.own), channel_id=1, source_target_pairs={{0,4},{8,12},{16,20},{24,28},{1,5},{9,13},{17,21},{25,29},{2,6},{1... | collective-permute-start | bytes 1572872 | tf_op jit(solution)/shard_map/ppermute | solution.py:702
  26.4 5.3 %collective-permute-start.2 = (bf16[256,1024]{1,0:T(8,128)(2,1)}, bf16[256,1024]{1,0:T(8,128)(2,1)}, u32[]{:S(2)}, u32[]{:S(2)}) collective-permute-start(bf16[256,1024]{1,0:T(8,128)(2,1)} %collective-permute-done.near_z), channel_id=1, source_target_pairs={{0,8},{4,12},{8,16},{12,20},{16,24},{20,28},{1,9},{5,13},{9,17},{1... | collective-permute-start | bytes 1572872 | tf_op jit(solution)/shard_map/ppermute | solution.py:702
  36.5 3.4 %shard_map.178 = (f32[256,4]{1,0:T(8,128)S(1)}, f32[256,4]{1,0:T(8,128)S(1)}, f32[4,256,128]{2,1,0:T(8,128)S(1)}) custom-call(s32[2]{0:T(128)S(1)} %copy-done.8, s32[8,256]{1,0:T(8,128)S(1)} %reshape.94.segments, s32[256,1]{1,0:T(8,128)S(1)} %copy.44.query_segment, bf16[256,512]{1,0:T(8,128)(2,1)S(1)} %copy-done.6, bf16[256,1024]{1,0:T(8,128)(2,1)S(1)} %copy-done.5, ...), custom_call_target="tpu_custom_call" | custom-call | flops 800000000 | bytes 4000000 | tf_op jit(solution)/shard_map/pallas_call | solution.py:372
  39.9 5.1 %collective-permute-done.1.cross = bf16[256,1024]{1,0:T(8,128)(2,1)S(1)} collective-permute-done((bf16[256,1024]{1,0:T(8,128)(2,1)}, bf16[256,1024]{1,0:T(8,128)(2,1)S(1)}, u32[]{:S(2)}, u32[]{:S(2)}) %collective-permute-start.1) | collective-permute-done | bytes 524320 | tf_op jit(solution)/shard_map/ppermute | solution.py:702
  45.1 5.5 %shard_map.179 = (bf16[128,2048]{1,0:T(8,128)(2,1)S(1)}, f32[128,2048]{1,0:T(8,128)S(1)}) custom-call(s32[2]{0:T(128)S(1)} %copy-done.8, s32[8,256]{1,0:T(8,128)S(1)} %reshape.94.segments, s32[256,1]{1,0:T(8,128)S(1)} %copy.44.query_segment, bf16[256,512]{1,0:T(8,128)(2,1)S(1)} %copy-done.6, bf16[256,1024]{1,0:T(8,128)(2,1)S(1)} %collective-permute-done.1.cross, ...), custom_call_target="tpu_custom_call" | custom-call | flops 1000000000 | bytes 6000000 | tf_op jit(solution)/shard_map/pallas_call | solution.py:380
  54.3 9.1 %collective-permute-start.7 = (f32[12,256]{1,0:T(8,128)S(1)}, f32[12,256]{1,0:T(8,128)S(1)}, u32[]{:S(2)}, u32[]{:S(2)}) collective-permute-start(f32[12,256]{1,0:T(8,128)S(1)} %get-tuple-element.67), channel_id=1, source_target_pairs={{0,4},{1,5},{2,6},{3,7},{4,0},{5,1},{6,2},{7,3},{8,12},{9,13},{10,... | collective-permute-start | bytes 36872 | tf_op jit(solution)/shard_map/ppermute | solution.py:242
  66.3 7.9 %collective-permute-start.11 = (bf16[64,2048]{1,0:T(8,128)(2,1)S(1)}, bf16[64,2048]{1,0:T(8,128)(2,1)S(1)}, u32[]{:S(2)}, u32[]{:S(2)}) collective-permute-start(bf16[64,2048]{1,0:T(8,128)(2,1)S(1)} %multiply_convert_fusion), channel_id=1, source_target_pairs={{0,8},{1,9},{2,10},{3,11},{4,12},{5,13},{6,14},{7,15},{8,24},{9,25... | collective-permute-start | bytes 786440 | tf_op jit(solution)/shard_map/ppermute | solution.py:242
  74.2 6.8 %collective-permute-done.11 = bf16[64,2048]{1,0:T(8,128)(2,1)S(1)} collective-permute-done((bf16[64,2048]{1,0:T(8,128)(2,1)S(1)}, bf16[64,2048]{1,0:T(8,128)(2,1)S(1)}, u32[]{:S(2)}, u32[]{:S(2)}) %collective-permute-start.11) | collective-permute-done | bytes 262176 | tf_op jit(solution)/shard_map/ppermute | solution.py:242
  81.9 3.4 %collective-permute-start.8 = (f32[2,12,256]{2,1,0:T(8,128)S(1)}, f32[2,12,256]{2,1,0:T(8,128)S(1)}, u32[]{:S(2)}, u32[]{:S(2)}) collective-permute-start(f32[2,12,256]{2,1,0:T(8,128)S(1)} %pad_maximum_fusion.1), channel_id=1, source_target_pairs={{0,8},{1,9},{2,10},{3,11},{4,12},{5,13},{6,14},{7,15},{8,24},{9,25... | collective-permute-start | bytes 73736 | tf_op jit(solution)/shard_map/ppermute | solution.py:242
  87.0 3.7 %collective-permute-done.8 = f32[2,12,256]{2,1,0:T(8,128)S(1)} collective-permute-done((f32[2,12,256]{2,1,0:T(8,128)S(1)}, f32[2,12,256]{2,1,0:T(8,128)S(1)}, u32[]{:S(2)}, u32[]{:S(2)}) %collective-permute-start.8) | collective-permute-done | bytes 24608 | tf_op jit(solution)/shard_map/ppermute | solution.py:242
  92.4 5.6 %collective-permute-done.29 = bf16[64,2048]{1,0:T(8,128)(2,1)S(1)} collective-permute-done((bf16[64,2048]{1,0:T(8,128)(2,1)S(1)}, bf16[64,2048]{1,0:T(8,128)(2,1)S(1)}, u32[]{:S(2)}, u32[]{:S(2)}) %collective-permute-start.29) | collective-permute-done | bytes 262176 | tf_op jit(solution)/shard_map/ppermute | solution.py:242
  106.9 4.8 %collective-permute-done.31.refs_6_ = bf16[128,2048]{1,0:T(8,128)(2,1)S(1)} collective-permute-done((bf16[128,2048]{1,0:T(8,128)(2,1)S(1)}, bf16[128,2048]{1,0:T(8,128)(2,1)S(1)}, u32[]{:S(2)}, u32[]{:S(2)}) %collective-permute-start.31) | collective-permute-done | bytes 524320 | tf_op jit(solution)/shard_map/ppermute | solution.py:242
  112.9 10.1 %collective-permute-done.14.refs_7_ = bf16[128,2048]{1,0:T(8,128)(2,1)} collective-permute-done((bf16[128,2048]{1,0:T(8,128)(2,1)}, bf16[128,2048]{1,0:T(8,128)(2,1)}, u32[]{:S(2)}, u32[]{:S(2)}) %collective-permute-start.14) | collective-permute-done | bytes 524320 | tf_op jit(solution)/shard_map/ppermute | solution.py:242
  131.4 27.2 %shard_map.181 = (bf16[128,2048]{1,0:T(8,128)(2,1)S(1)}, bf16[128,2048]{1,0:T(8,128)(2,1)S(1)}, bf16[128,2048]{1,0:T(8,128)(2,1)S(1)}, bf16[128,2048]{1,0:T(8,12...) custom-call(s32[2]{0:T(128)S(1)} %copy-done.8, ...), custom_call_target="tpu_custom_call" | custom-call | flops 10000000000 | bytes 44000000 | tf_op jit(solution)/shard_map/pallas_call | solution.py:608
  159.6 27.8 %shard_map.182 = (bf16[128,2048]{1,0:T(8,128)(2,1)S(1)}, bf16[128,2048]{1,0:T(8,128)(2,1)S(1)}, bf16[128,2048]{1,0:T(8,128)(2,1)S(1)}, bf16[128,2048]{1,0:T(8,12...) custom-call(s32[2]{0:T(128)S(1)} %copy-done.8, ...), custom_call_target="tpu_custom_call" | custom-call | flops 10000000000 | bytes 44000000 | tf_op jit(solution)/shard_map/pallas_call | solution.py:608
  193.1 8.8 %collective-permute-done.21 = bf16[128,2048]{1,0:T(8,128)(2,1)S(1)} collective-permute-done((bf16[128,2048]{1,0:T(8,128)(2,1)S(1)}, bf16[128,2048]{1,0:T(8,128)(2,1)S(1)}, u32[]{:S(2)}, u32[]{:S(2)}) %collective-permute-start.21) | collective-permute-done | bytes 524320 | tf_op jit(solution)/shard_map/ppermute | solution.py:242
  205.6 8.3 %collective-permute-done.43 = bf16[128,2048]{1,0:T(8,128)(2,1)S(1)} collective-permute-done((bf16[128,2048]{1,0:T(8,128)(2,1)S(1)}, bf16[128,2048]{1,0:T(8,128)(2,1)S(1)}, u32[]{:S(2)}, u32[]{:S(2)}) %collective-permute-start.43) | collective-permute-done | bytes 524320 | tf_op jit(solution)/shard_map/ppermute | solution.py:242
  216.0 4.0 %collective-permute-done.26 = bf16[128,2048]{1,0:T(8,128)(2,1)S(1)} collective-permute-done((bf16[128,2048]{1,0:T(8,128)(2,1)S(1)}, bf16[128,2048]{1,0:T(8,128)(2,1)S(1)}, u32[]{:S(2)}, u32[]{:S(2)}) %collective-permute-start.26) | collective-permute-done | bytes 524320 | tf_op jit(solution)/shard_map/ppermute | solution.py:242
  222.2 3.5 %collective-permute-done.44 = bf16[128,2048]{1,0:T(8,128)(2,1)S(1)} collective-permute-done((bf16[128,2048]{1,0:T(8,128)(2,1)S(1)}, bf16[128,2048]{1,0:T(8,128)(2,1)S(1)}, u32[]{:S(2)}, u32[]{:S(2)}) %collective-permute-start.44) | collective-permute-done | bytes 524320 | tf_op jit(solution)/shard_map/ppermute | solution.py:242
  226.0 4.1 %collective-permute-start.45 = (bf16[64,2048]{1,0:T(8,128)(2,1)S(1)}, bf16[64,2048]{1,0:T(8,128)(2,1)S(1)}, u32[]{:S(2)}, u32[]{:S(2)}) collective-permute-start(bf16[64,2048]{1,0:T(8,128)(2,1)S(1)} %get-tuple-element.62), channel_id=1, source_target_pairs={{0,24},{1,25},{2,26},{3,27},{4,28},{5,29},{6,30},{7,31},{8,16},{9,... | collective-permute-start | bytes 786440 | tf_op jit(solution)/shard_map/ppermute | solution.py:242
  230.2 7.2 %collective-permute-done.45 = bf16[64,2048]{1,0:T(8,128)(2,1)S(1)} collective-permute-done((bf16[64,2048]{1,0:T(8,128)(2,1)S(1)}, bf16[64,2048]{1,0:T(8,128)(2,1)S(1)}, u32[]{:S(2)}, u32[]{:S(2)}) %collective-permute-start.45) | collective-permute-done | bytes 262176 | tf_op jit(solution)/shard_map/ppermute | solution.py:242
  237.4 9.7 %collective-permute-done.46 = bf16[64,2048]{1,0:T(8,128)(2,1)S(1)} collective-permute-done((bf16[64,2048]{1,0:T(8,128)(2,1)S(1)}, bf16[64,2048]{1,0:T(8,128)(2,1)S(1)}, u32[]{:S(2)}, u32[]{:S(2)}) %collective-permute-start.46) | collective-permute-done | bytes 262176 | tf_op jit(solution)/shard_map/ppermute | solution.py:242
  (170 shorter events, 54.9 us)
Async XLA Ops:
  3.4 16.4 %collective-permute-start = (bf16[256,1024]{1,0:T(8,128)(2,1)}, bf16[256,1024]{1,0:T(8,128)(2,1)}, u32[]{:S(2)}, u32[]{:S(2)}) collective-permute-start(bf16[256,1024]{1,0:T(8,128)(2,1)} %get-tuple-element.33.refs_6_.own), channel_id=1, source_target_pairs={{0,8},{4,12},{8,16},{12,20},{16,24},{20,28},{1,9},{5,13},{9,17},{1... | collective-permute-start | bytes 1572872 | tf_op jit(solution)/shard_map/ppermute | solution.py:702
  19.8 16.1 %collective-permute-start.4 = (bf16[256,1024]{1,0:T(8,128)(2,1)}, bf16[256,1024]{1,0:T(8,128)(2,1)}, u32[]{:S(2)}, u32[]{:S(2)}) collective-permute-start(bf16[256,1024]{1,0:T(8,128)(2,1)} %get-tuple-element.33.refs_6_.own), channel_id=1, source_target_pairs={{0,4},{8,12},{16,20},{24,28},{1,5},{9,13},{17,21},{25,29},{2,6},{1... | collective-permute-start | bytes 1572872 | tf_op jit(solution)/shard_map/ppermute | solution.py:702
  26.3 18.7 %collective-permute-start.1 = (bf16[256,1024]{1,0:T(8,128)(2,1)}, bf16[256,1024]{1,0:T(8,128)(2,1)S(1)}, u32[]{:S(2)}, u32[]{:S(2)}) collective-permute-start(bf16[256,1024]{1,0:T(8,128)(2,1)} %collective-permute-done.near_z), channel_id=1, source_target_pairs={{0,4},{4,0},{8,12},{12,8},{16,20},{20,16},{24,28},{28,24},{1,5},{5... | collective-permute-start | bytes 1572872 | tf_op jit(solution)/shard_map/ppermute | solution.py:702
  26.4 18.6 %collective-permute-start.2 = (bf16[256,1024]{1,0:T(8,128)(2,1)}, bf16[256,1024]{1,0:T(8,128)(2,1)}, u32[]{:S(2)}, u32[]{:S(2)}) collective-permute-start(bf16[256,1024]{1,0:T(8,128)(2,1)} %collective-permute-done.near_z), channel_id=1, source_target_pairs={{0,8},{4,12},{8,16},{12,20},{16,24},{20,28},{1,9},{5,13},{9,17},{1... | collective-permute-start | bytes 1572872 | tf_op jit(solution)/shard_map/ppermute | solution.py:702
  54.3 27.5 %collective-permute-start.7 = (f32[12,256]{1,0:T(8,128)S(1)}, f32[12,256]{1,0:T(8,128)S(1)}, u32[]{:S(2)}, u32[]{:S(2)}) collective-permute-start(f32[12,256]{1,0:T(8,128)S(1)} %get-tuple-element.67), channel_id=1, source_target_pairs={{0,4},{1,5},{2,6},{3,7},{4,0},{5,1},{6,2},{7,3},{8,12},{9,13},{10,... | collective-permute-start | bytes 36872 | tf_op jit(solution)/shard_map/ppermute | solution.py:242
  66.3 14.7 %collective-permute-start.11 = (bf16[64,2048]{1,0:T(8,128)(2,1)S(1)}, bf16[64,2048]{1,0:T(8,128)(2,1)S(1)}, u32[]{:S(2)}, u32[]{:S(2)}) collective-permute-start(bf16[64,2048]{1,0:T(8,128)(2,1)S(1)} %multiply_convert_fusion), channel_id=1, source_target_pairs={{0,8},{1,9},{2,10},{3,11},{4,12},{5,13},{6,14},{7,15},{8,24},{9,25... | collective-permute-start | bytes 786440 | tf_op jit(solution)/shard_map/ppermute | solution.py:242
  100.1 22.9 %collective-permute-start.14 = (bf16[128,2048]{1,0:T(8,128)(2,1)}, bf16[128,2048]{1,0:T(8,128)(2,1)}, u32[]{:S(2)}, u32[]{:S(2)}) collective-permute-start(bf16[128,2048]{1,0:T(8,128)(2,1)} %collective-permute-done.12.refs_5_), channel_id=1, source_target_pairs={{0,4},{1,3},{2,6},{3,1},{4,0},{5,7},{6,2},{7,5},{8,12},{9,11},{10,... | collective-permute-start | bytes 1572872 | tf_op jit(solution)/shard_map/ppermute | solution.py:242
  100.2 22.8 %collective-permute-start.15 = (bf16[128,2048]{1,0:T(8,128)(2,1)}, bf16[128,2048]{1,0:T(8,128)(2,1)}, u32[]{:S(2)}, u32[]{:S(2)}) collective-permute-start(bf16[128,2048]{1,0:T(8,128)(2,1)} %collective-permute-done.13.refs_6_), channel_id=1, source_target_pairs={{0,2},{1,5},{2,0},{3,7},{4,6},{5,1},{6,4},{7,3},{8,10},{9,13},{10,... | collective-permute-start | bytes 1572872 | tf_op jit(solution)/shard_map/ppermute | solution.py:242
  104.8 26.0 %collective-permute-start.16 = (bf16[128,2048]{1,0:T(8,128)(2,1)}, bf16[128,2048]{1,0:T(8,128)(2,1)}, u32[]{:S(2)}, u32[]{:S(2)}) collective-permute-start(bf16[128,2048]{1,0:T(8,128)(2,1)} %collective-permute-done.13.refs_6_), channel_id=1, source_target_pairs={{0,1},{1,0},{2,3},{3,2},{4,5},{5,4},{6,7},{7,6},{8,9},{9,8},{10,11... | collective-permute-start | bytes 1572872 | tf_op jit(solution)/shard_map/ppermute | solution.py:242
  104.9 25.9 %collective-permute-start.32 = (bf16[128,2048]{1,0:T(8,128)(2,1)S(1)}, bf16[128,2048]{1,0:T(8,128)(2,1)S(1)}, u32[]{:S(2)}, u32[]{:S(2)}) collective-permute-start(bf16[128,2048]{1,0:T(8,128)(2,1)S(1)} %collective-permute-done.30.refs_5_), channel_id=1, source_target_pairs={{0,4},{1,3},{2,6},{3,1},{4,0},{5,7},{6,2},{7,5},{8,12},{9,11},{10,... | collective-permute-start | bytes 1572872 | tf_op jit(solution)/shard_map/ppermute | solution.py:242
  111.7 19.6 %collective-permute-start.33 = (bf16[128,2048]{1,0:T(8,128)(2,1)S(1)}, bf16[128,2048]{1,0:T(8,128)(2,1)S(1)}, u32[]{:S(2)}, u32[]{:S(2)}) collective-permute-start(bf16[128,2048]{1,0:T(8,128)(2,1)S(1)} %collective-permute-done.31.refs_6_), channel_id=1, source_target_pairs={{0,2},{1,5},{2,0},{3,7},{4,6},{5,1},{6,4},{7,3},{8,10},{9,13},{10,... | collective-permute-start | bytes 1572872 | tf_op jit(solution)/shard_map/ppermute | solution.py:242
  130.8 28.4 %collective-permute-start.34 = (bf16[128,2048]{1,0:T(8,128)(2,1)S(1)}, bf16[128,2048]{1,0:T(8,128)(2,1)S(1)}, u32[]{:S(2)}, u32[]{:S(2)}) collective-permute-start(bf16[128,2048]{1,0:T(8,128)(2,1)S(1)} %collective-permute-done.31.refs_6_), channel_id=1, source_target_pairs={{0,1},{1,0},{2,3},{3,2},{4,5},{5,4},{6,7},{7,6},{8,9},{9,8},{10,11... | collective-permute-start | bytes 1572872 | tf_op jit(solution)/shard_map/ppermute | solution.py:242
  130.8 28.8 %collective-permute-start.35 = (bf16[128,2048]{1,0:T(8,128)(2,1)S(1)}, bf16[128,2048]{1,0:T(8,128)(2,1)S(1)}, u32[]{:S(2)}, u32[]{:S(2)}) collective-permute-start(bf16[128,2048]{1,0:T(8,128)(2,1)S(1)} %collective-permute-done.32.refs_7_), channel_id=1, source_target_pairs={{0,1},{1,0},{2,3},{3,2},{4,5},{5,4},{6,7},{7,6},{8,9},{9,8},{10,11... | collective-permute-start | bytes 1572872 | tf_op jit(solution)/shard_map/ppermute | solution.py:242
  131.3 28.3 %collective-permute-start.36 = (bf16[128,2048]{1,0:T(8,128)(2,1)S(1)}, bf16[128,2048]{1,0:T(8,128)(2,1)S(1)}, u32[]{:S(2)}, u32[]{:S(2)}) collective-permute-start(bf16[128,2048]{1,0:T(8,128)(2,1)S(1)} %collective-permute-done.33.refs_8_), channel_id=1, source_target_pairs={{0,1},{1,0},{2,3},{3,2},{4,5},{5,4},{6,7},{7,6},{8,9},{9,8},{10,11... | collective-permute-start | bytes 1572872 | tf_op jit(solution)/shard_map/ppermute | solution.py:242
  158.5 29.5 %collective-permute-start.20 = (bf16[128,2048]{1,0:T(8,128)(2,1)S(1)}, bf16[128,2048]{1,0:T(8,128)(2,1)S(1)}, u32[]{:S(2)}, u32[]{:S(2)}) collective-permute-start(bf16[128,2048]{1,0:T(8,128)(2,1)S(1)} %get-tuple-element.46), channel_id=1, source_target_pairs={{0,1},{1,0},{2,3},{3,2},{4,5},{5,4},{6,7},{7,6},{8,9},{9,8},{10,11... | collective-permute-start | bytes 1572872 | tf_op jit(solution)/shard_map/ppermute | solution.py:242
  159.0 29.2 %collective-permute-start.24 = (bf16[128,2048]{1,0:T(8,128)(2,1)}, bf16[128,2048]{1,0:T(8,128)(2,1)S(1)}, u32[]{:S(2)}, u32[]{:S(2)}) collective-permute-start(bf16[128,2048]{1,0:T(8,128)(2,1)} %get-tuple-element.50), channel_id=1, source_target_pairs={{0,1},{1,0},{2,3},{3,2},{4,5},{5,4},{6,7},{7,6},{8,9},{9,8},{10,11... | collective-permute-start | bytes 1572872 | tf_op jit(solution)/shard_map/ppermute | solution.py:242
  159.1 33.8 %collective-permute-start.23 = (bf16[128,2048]{1,0:T(8,128)(2,1)S(1)}, bf16[128,2048]{1,0:T(8,128)(2,1)S(1)}, u32[]{:S(2)}, u32[]{:S(2)}) collective-permute-start(bf16[128,2048]{1,0:T(8,128)(2,1)S(1)} %get-tuple-element.48), channel_id=1, source_target_pairs={{0,1},{1,0},{2,3},{3,2},{4,5},{5,4},{6,7},{7,6},{8,9},{9,8},{10,11... | collective-permute-start | bytes 1572872 | tf_op jit(solution)/shard_map/ppermute | solution.py:242
  188.0 16.4 %collective-permute-start.41 = (bf16[128,2048]{1,0:T(8,128)(2,1)S(1)}, bf16[128,2048]{1,0:T(8,128)(2,1)S(1)}, u32[]{:S(2)}, u32[]{:S(2)}) collective-permute-start(bf16[128,2048]{1,0:T(8,128)(2,1)S(1)} %get-tuple-element.56), channel_id=1, source_target_pairs={{0,1},{1,0},{2,3},{3,2},{4,5},{5,4},{6,7},{7,6},{8,9},{9,8},{10,11... | collective-permute-start | bytes 1572872 | tf_op jit(solution)/shard_map/ppermute | solution.py:242
  190.5 13.6 %collective-permute-start.25 = (bf16[128,2048]{1,0:T(8,128)(2,1)S(1)}, bf16[128,2048]{1,0:T(8,128)(2,1)S(1)}, u32[]{:S(2)}, u32[]{:S(2)}) collective-permute-start(bf16[128,2048]{1,0:T(8,128)(2,1)S(1)} %add_convert_fusion.5), channel_id=1, source_target_pairs={{0,2},{1,5},{2,0},{3,7},{4,6},{5,1},{6,4},{7,3},{8,10},{9,13},{10,... | collective-permute-start | bytes 1572872 | tf_op jit(solution)/shard_map/ppermute | solution.py:242
  192.3 21.7 %collective-permute-start.43 = (bf16[128,2048]{1,0:T(8,128)(2,1)S(1)}, bf16[128,2048]{1,0:T(8,128)(2,1)S(1)}, u32[]{:S(2)}, u32[]{:S(2)}) collective-permute-start(bf16[128,2048]{1,0:T(8,128)(2,1)S(1)} %add_convert_fusion.2), channel_id=1, source_target_pairs={{0,2},{1,5},{2,0},{3,7},{4,6},{5,1},{6,4},{7,3},{8,10},{9,13},{10,... | collective-permute-start | bytes 1572872 | tf_op jit(solution)/shard_map/ppermute | solution.py:242
  193.0 21.2 %collective-permute-start.19 = (bf16[128,2048]{1,0:T(8,128)(2,1)S(1)}, bf16[128,2048]{1,0:T(8,128)(2,1)S(1)}, u32[]{:S(2)}, u32[]{:S(2)}) collective-permute-start(bf16[128,2048]{1,0:T(8,128)(2,1)S(1)} %get-tuple-element.44), channel_id=1, source_target_pairs={{0,1},{1,0},{2,3},{3,2},{4,5},{5,4},{6,7},{7,6},{8,9},{9,8},{10,11... | collective-permute-start | bytes 1572872 | tf_op jit(solution)/shard_map/ppermute | solution.py:242
  201.8 14.1 %collective-permute-start.39 = (bf16[128,2048]{1,0:T(8,128)(2,1)S(1)}, bf16[128,2048]{1,0:T(8,128)(2,1)S(1)}, u32[]{:S(2)}, u32[]{:S(2)}) collective-permute-start(bf16[128,2048]{1,0:T(8,128)(2,1)S(1)} %add_convert_fusion.3), channel_id=1, source_target_pairs={{0,4},{1,3},{2,6},{3,1},{4,0},{5,7},{6,2},{7,5},{8,12},{9,11},{10,... | collective-permute-start | bytes 1572872 | tf_op jit(solution)/shard_map/ppermute | solution.py:242
  204.4 15.6 %collective-permute-start.26 = (bf16[128,2048]{1,0:T(8,128)(2,1)S(1)}, bf16[128,2048]{1,0:T(8,128)(2,1)S(1)}, u32[]{:S(2)}, u32[]{:S(2)}) collective-permute-start(bf16[128,2048]{1,0:T(8,128)(2,1)S(1)} %add_convert_fusion.4), channel_id=1, source_target_pairs={{0,4},{1,3},{2,6},{3,1},{4,0},{5,7},{6,2},{7,5},{8,12},{9,11},{10,... | collective-permute-start | bytes 1572872 | tf_op jit(solution)/shard_map/ppermute | solution.py:242
  230.2 16.9 %collective-permute-start.46 = (bf16[64,2048]{1,0:T(8,128)(2,1)S(1)}, bf16[64,2048]{1,0:T(8,128)(2,1)S(1)}, u32[]{:S(2)}, u32[]{:S(2)}) collective-permute-start(bf16[64,2048]{1,0:T(8,128)(2,1)S(1)} %get-tuple-element.63), channel_id=1, source_target_pairs={{0,8},{1,9},{2,10},{3,11},{4,12},{5,13},{6,14},{7,15},{8,24},{9,25... | collective-permute-start | bytes 786440 | tf_op jit(solution)/shard_map/ppermute | solution.py:242
  (39 other events, 428.8 us)

commit v2 on v1

--- a/solution.py
+++ b/solution.py
@@ -221,20 +221,22 @@
 
 
 def slice_order():
-    order = np.zeros((4, 2, 16), np.int32)
-    for y in range(2):
-        for c in range(2):
-            mine = {
-                0: [(1, y, 0), (1, y, 1), (1, 1 - y, 0)],
-                1: [(0, 1 - y, 1), (0, 1 - y, 0), (1, 1 - y, 1)],
-            }
-            places = [(0, y, c), (0, y, 1 - c)] + mine[c] + mine[1 - c]
-            for group in range(2):
-                order[y * 2 + c, group] = [
-                    ((2 * group + part) * 2 + other) * 4 + at_y * 2 + at_c
-                    for other, at_y, at_c in places
-                    for part in range(2)
-                ]
+    order = np.zeros((len(DEVICES), 32), np.int32)
+    for z, x, y, c in DEVICES:
+        at_step = [z]
+        for _ in range(3):
+            at_step.append(BACK_Z[at_step[-1]])
+        mine = {
+            0: [(1 - x, y, 0), (1 - x, y, 1), (1 - x, 1 - y, 0)],
+            1: [(x, 1 - y, 1), (x, 1 - y, 0), (1 - x, 1 - y, 1)],
+        }
+        places = [(x, y, c), (x, y, 1 - c)] + mine[c] + mine[1 - c]
+        order[flat_index(z, x, y, c)] = [
+            flat_index(at_step[2 * group + part], *place)
+            for group in range(2)
+            for place in places
+            for part in range(2)
+        ]
     return order
 
 
@@ -310,7 +312,7 @@
 
 
 def attention_first(
-    place, segments, query_segment, queries, own, near_x, near_z, after, top, total, mixed
+    place, segments, query_segment, queries, own, near_x, near_z, top, total, mixed
 ):
     here = place[0]
     blocks = [(own, here), (near_x, jnp.where(here % 2 == 1, here - 1, -1)), (near_z, here - 2)]
@@ -323,7 +325,7 @@
 
 def attention_second(
     place, segments, query_segment, queries, cross, far, far_cross, projection,
-    top, total, mixed, after, sent, kept, attended,
+    top, total, mixed, sent, kept, attended,
 ):
     here, hd = place[0], place[1]
     odd = here % 2
@@ -359,7 +361,7 @@
 
 
 def attention(
-    place, segment_ids, query_segment, queries, own, near_x, near_z, cross, far, far_cross, out_proj, after
+    place, segment_ids, query_segment, queries, own, near_x, near_z, cross, far, far_cross, out_proj
 ):
     segments = segment_ids.reshape(-1, BLOCK)
     state = (
@@ -367,57 +369,30 @@
         jax.ShapeDtypeStruct((BLOCK, HEADS_HERE), jnp.float32),
         jax.ShapeDtypeStruct((HEADS_HERE, BLOCK, HD), jnp.float32),
     )
-    smem, vmem, anywhere = whole(pltpu.SMEM), whole(), whole(pl.ANY)
+    smem, vmem = whole(pltpu.SMEM), whole()
     limit = pltpu.CompilerParams(vmem_limit_bytes=24 * 2**20)
     first = pl.pallas_call(
         attention_first,
         out_shape=state,
-        in_specs=[smem] + [vmem] * 6 + [anywhere],
+        in_specs=[smem] + [vmem] * 6,
         out_specs=(vmem, vmem, vmem),
         compiler_params=limit,
         cost_estimate=pl.CostEstimate(flops=8 * 10**8, bytes_accessed=4 * 10**6, transcendentals=8 * 10**5),
-    )(place, segments, query_segment, queries, own, near_x, near_z, after[0])
+    )(place, segments, query_segment, queries, own, near_x, near_z)
     return pl.pallas_call(
         attention_second,
         out_shape=(
             jax.ShapeDtypeStruct((2 * ROWS, out_proj.shape[1]), jnp.bfloat16),
             jax.ShapeDtypeStruct((2 * ROWS, out_proj.shape[1]), jnp.float32),
         ),
-        in_specs=[smem] + [vmem] * 10 + [anywhere],
+        in_specs=[smem] + [vmem] * 10,
         out_specs=(vmem, vmem),
         scratch_shapes=[pltpu.VMEM((BLOCK, HEADS_HERE * HD), jnp.bfloat16)],
         compiler_params=limit,
         cost_estimate=pl.CostEstimate(flops=10**9, bytes_accessed=6 * 10**6, transcendentals=8 * 10**5),
     )(
-        place, segments, query_segment, queries, cross, far, far_cross, out_proj, *first, after[1]
-    )
-
-
-def touch(arrays, after):
-    count = len(arrays)
-
-    def kernel(*refs):
-        sources, token, strips, arrived = refs[:count], refs[count + 1], refs[count + 2 : -1], refs[-1]
-        copies = [
-            pltpu.make_async_copy(source.at[:, pl.ds(0, HD)], strip, arrived.at[number])
-            for number, (source, strip) in enumerate(zip(sources, strips))
-        ]
-        for copy in copies:
-            copy.start()
-        token[...] = jnp.zeros_like(token)
-        for copy in copies:
-            copy.wait()
-
-    return pl.pallas_call(
-        kernel,
-        out_shape=jax.ShapeDtypeStruct((8, HD), jnp.float32),
-        in_specs=[whole(pltpu.HBM)] * count + [whole(pl.ANY)],
-        out_specs=whole(),
-        scratch_shapes=[pltpu.VMEM((array.shape[0], HD), array.dtype) for array in arrays]
-        + [pltpu.SemaphoreType.DMA((count,))],
-        compiler_params=pltpu.CompilerParams(vmem_limit_bytes=58 * 2**20),
-        cost_estimate=pl.CostEstimate(flops=0, bytes_accessed=3 * 10**6, transcendentals=0),
-    )(*arrays, after)
+        place, segments, query_segment, queries, cross, far, far_cross, out_proj, *first
+    )
 
 
 CHUNK = 256
@@ -431,45 +406,49 @@
     return (gate_val / (1.0 + jnp.exp(-gate_val)) * up_val).astype(jnp.bfloat16)
 
 
-def routing_kernel(slot_row, weight_row, slot_column, pick, spread, slot_weight):
-    slot_numbers = lax.broadcasted_iota(jnp.int32, (SLOTS, GROUP_ROWS), 0)
-    slot_lanes = lax.broadcasted_iota(jnp.int32, (GROUP_ROWS, 2 * SLOTS), 1)
+def routing_kernel(place, order, slices, pick, spread, slot_weight, listed):
+    count = slices.shape[1] // 2
+    for number in range(32):
+        listed[:, number * ROWS : (number + 1) * ROWS] = slices[order[number]]
+    first_expert = (2 * (place[0] * 4 + place[1])).astype(jnp.float32)
+    hits, weights = [], []
+    for group in range(2):
+        lanes = slice(group * GROUP_ROWS, (group + 1) * GROUP_ROWS)
+        for expert in range(2):
+            match = listed[:count, lanes] == first_expert + float(expert)
+            hits.append(jnp.max(jnp.where(match, 1.0, 0.0), axis=0, keepdims=True))
+            weights.append(jnp.sum(jnp.where(match, listed[count:, lanes], 0.0), axis=0, keepdims=True))
+    hits = jnp.concatenate(hits + hits, axis=0)
+    earlier = lax.broadcasted_iota(jnp.int32, (GROUP_ROWS, GROUP_ROWS), 0) < lax.broadcasted_iota(
+        jnp.int32, (GROUP_ROWS, GROUP_ROWS), 1
+    )
+    before = jnp.dot(
+        hits.astype(jnp.bfloat16),
+        jnp.where(earlier, 1.0, 0.0).astype(jnp.bfloat16),
+        preferred_element_type=jnp.float32,
+    )
+    slot = jnp.where(hits > 0.0, before, -1.0)
+    slot_column = slot.T
+    slot_numbers = lax.broadcasted_iota(jnp.int32, (SLOTS, GROUP_ROWS), 0).astype(jnp.float32)
+    slot_lanes = lax.broadcasted_iota(jnp.int32, (GROUP_ROWS, 2 * SLOTS), 1).astype(jnp.float32)
     for group in range(2):
         for expert in range(2):
-            line = slice(2 * group + expert, 2 * group + expert + 1)
+            line = 2 * group + expert
             held = slice(expert * SLOTS, (expert + 1) * SLOTS)
-            hit = slot_row[line, :] == slot_numbers
+            hit = slot[line : line + 1] == slot_numbers
             pick[group, held] = jnp.where(hit, 1.0, 0.0).astype(jnp.bfloat16)
-            slot_weight[group, held] = jnp.sum(
-                jnp.where(hit, weight_row[line, :], 0.0), axis=1, keepdims=True
-            )
+            slot_weight[group, held] = jnp.sum(jnp.where(hit, weights[line], 0.0), axis=1, keepdims=True)
         first, second = [slot_column[:, 2 * group + e : 2 * group + e + 1] for e in range(2)]
-        hit = (first == slot_lanes) | ((second >= 0) & (second + SLOTS == slot_lanes))
+        hit = (first == slot_lanes) | ((second >= 0.0) & (second + float(SLOTS) == slot_lanes))
         spread[group] = jnp.where(hit, 1.0, 0.0).astype(jnp.bfloat16)
 
 
-def routing_matrices(slot, weight):
-    return pl.pallas_call(
-        routing_kernel,
-        out_shape=(
-            jax.ShapeDtypeStruct((2, 2 * SLOTS, GROUP_ROWS), jnp.bfloat16),
-            jax.ShapeDtypeStruct((2, GROUP_ROWS, 2 * SLOTS), jnp.bfloat16),
-            jax.ShapeDtypeStruct((2, 2 * SLOTS, 1), jnp.float32),
-        ),
-        in_specs=[whole()] * 3,
-        out_specs=(whole(),) * 3,
-        compiler_params=pltpu.CompilerParams(vmem_limit_bytes=16 * 2**20),
-    )(slot, weight, slot.T)
-
-
-def experts_kernel(group, with_shared, *refs):
+def experts_kernel(*refs):
     place, pick, spread, slot_weight = refs[:4]
-    pieces, refs = refs[4 : 4 + PIECES], refs[4 + PIECES :]
+    pieces, refs = refs[4 : 4 + 2 * PIECES], refs[4 + 2 * PIECES :]
     gate, up, down = refs[:3]
-    refs = refs[3:]
-    if with_shared:
-        shared, refs = refs[:3], refs[3:]
-    targets, refs = refs[:PIECES], refs[PIECES:]
+    shared = refs[3:6]
+    targets, refs = refs[6 : 6 + 2 * PIECES], refs[6 + 2 * PIECES :]
     rows, picked, hidden, gate_held, up_held, down_held, arrived, gate_up_arrived, down_arrived = refs[:9]
     width = rows.shape[1]
     chunks = [
@@ -501,22 +480,29 @@
         for copy in gate_up_copies(number):
             copy.start()
     down_copy(0).start()
-    if with_shared:
-        s_gate, s_up, s_down, s_arrived, s_rows, s_hidden = refs[9:]
-        s_copies = [
-            pltpu.make_async_copy(source, target, s_arrived.at[number])
-            for number, (source, target) in enumerate(zip(shared, (s_gate, s_up, s_down)))
-        ]
-
-    for copy in copies:
-        copy.wait()
-    for low in range(0, width, WIDE):
-        lanes = slice(low, low + WIDE)
-        picked[:, lanes] = jnp.dot(
-            pick[group], rows[:, lanes], preferred_element_type=jnp.float32
-        ).astype(jnp.bfloat16)
+    s_gate, s_up, s_down, s_arrived, s_rows, s_hidden = refs[9:]
+    s_copies = [
+        pltpu.make_async_copy(source, target, s_arrived.at[number])
+        for number, (source, target) in enumerate(zip(shared, (s_gate, s_up, s_down)))
+    ]
+
+    def slots(expert, group):
+        return slice((2 * expert + group) * SLOTS, (2 * expert + group + 1) * SLOTS)
+
+    for group in range(2):
+        for copy in copies[group * PIECES : (group + 1) * PIECES]:
+            copy.wait()
+        for low in range(0, width, WIDE):
+            lanes = slice(low, low + WIDE)
+            both = jnp.dot(
+                pick[group],
+                rows[group * GROUP_ROWS : (group + 1) * GROUP_ROWS, lanes],
+                preferred_element_type=jnp.float32,
+            ).astype(jnp.bfloat16)
+            for expert in range(2):
+                picked[slots(expert, group), lanes] = both[expert * SLOTS : (expert + 1) * SLOTS]
     for number, (expert, low, size) in enumerate(chunks):
-        held, slot = slice(expert * SLOTS, (expert + 1) * SLOTS), number % DEPTH
+        held, slot = slice(2 * expert * SLOTS, 2 * (expert + 1) * SLOTS), number % DEPTH
         for copy in gate_up_copies(number):
             copy.wait()
         gate_val = jnp.dot(picked[held], gate_held[slot, :, :size], preferred_element_type=jnp.float32)
@@ -527,98 +513,97 @@
                 copy.start()
         if number == len(chunks) // 2:
             down_copy(1).start()
-        if with_shared and number == len(chunks) - DEPTH:
+        if number == len(chunks) - DEPTH:
             for copy in s_copies:
                 copy.start()
         if low + size == FF_E:
             down_copy(expert).wait()
+            scale = jnp.concatenate(
+                [slot_weight[group, expert * SLOTS : (expert + 1) * SLOTS] for group in range(2)], axis=0
+            )
             for start in range(0, width, WIDE):
                 lanes = slice(start, start + WIDE)
                 result = jnp.dot(
                     hidden[...], down_held[expert, :, lanes], preferred_element_type=jnp.float32
                 )
-                picked[held, lanes] = (result * slot_weight[group, held]).astype(jnp.bfloat16)
-
-    if with_shared:
-        upper = place[1] % 2 == 1
-        s_rows[0:ROWS] = rows[0:ROWS]
-        s_rows[ROWS : 2 * ROWS] = rows[PIECE : PIECE + ROWS]
-        base = pl.multiple_of(jnp.where(upper, 2, 5) * PIECE, PIECE)
-        s_rows[2 * ROWS : 3 * ROWS] = rows[pl.ds(base, ROWS), :]
-        s_rows[3 * ROWS : 4 * ROWS] = rows[pl.ds(base + PIECE, ROWS), :]
-        for copy in s_copies:
-            copy.wait()
-        turned = (((1,), (1,)), ((), ()))
-        units = s_gate.shape[0]
-        for low in range(0, units, CHUNK):
-            size = min(CHUNK, units - low)
-            gate_val, up_val = [
-                lax.dot_general(
-                    s_rows[...], weight[low : low + size, :], turned, preferred_element_type=jnp.float32
-                )
-                for weight in (s_gate, s_up)
-            ]
-            s_hidden[:, low : low + size] = silu_times(gate_val, up_val)
+                picked[held, lanes] = (result * scale).astype(jnp.bfloat16)
+
+    upper = place[1] % 2 == 1
+    s_rows[0:ROWS] = rows[0:ROWS]
+    s_rows[ROWS : 2 * ROWS] = rows[PIECE : PIECE + ROWS]
+    base = pl.multiple_of(jnp.where(upper, 2, 5) * PIECE, PIECE)
+    s_rows[2 * ROWS : 3 * ROWS] = rows[pl.ds(base, ROWS), :]
+    s_rows[3 * ROWS : 4 * ROWS] = rows[pl.ds(base + PIECE, ROWS), :]
+    for copy in s_copies:
+        copy.wait()
+    turned = (((1,), (1,)), ((), ()))
+    units = s_gate.shape[0]
+    for low in range(0, units, CHUNK):
+        size = min(CHUNK, units - low)
+        gate_val, up_val = [
+            lax.dot_general(
+                s_rows[...], weight[low : low + size, :], turned, preferred_element_type=jnp.float32
+            )
+            for weight in (s_gate, s_up)
+        ]
+        s_hidden[:, low : low + size] = silu_times(gate_val, up_val)
 
     for low in range(0, width, CHUNK):
         lanes = slice(low, low + CHUNK)
-        value = jnp.dot(spread[group], picked[:, lanes], preferred_element_type=jnp.float32)
-        if with_shared:
-            s_result = jnp.dot(s_hidden[...], s_down[:, lanes], preferred_element_type=jnp.float32)
-        for part, target in enumerate(targets):
-            mine = value[part * PIECE : (part + 1) * PIECE]
-            if with_shared and part in (0, 1, 2, 3, 5, 6):
-                if part < 2:
-                    term = s_result[part * ROWS : (part + 1) * ROWS]
+        s_result = jnp.dot(s_hidden[...], s_down[:, lanes], preferred_element_type=jnp.float32)
+        for group in range(2):
+            value = jnp.dot(
+                spread[group],
+                jnp.concatenate([picked[slots(expert, group), lanes] for expert in range(2)], axis=0),
+                preferred_element_type=jnp.float32,
+            )
+            for part, target in enumerate(targets[group * PIECES : (group + 1) * PIECES]):
+                mine = value[part * PIECE : (part + 1) * PIECE]
+                if group == 0 and part in (0, 1, 2, 3, 5, 6):
+                    if part < 2:
+                        term = s_result[part * ROWS : (part + 1) * ROWS]
+                    else:
+                        start = (2 + (part - 2) % 3) * ROWS
+                        here = upper if part < 4 else jnp.logical_not(upper)
+                        term = jnp.where(here, s_result[start : start + ROWS], 0.0)
+                    target[:ROWS, lanes] = (mine[:ROWS] + term).astype(jnp.bfloat16)
+                    target[ROWS:, lanes] = mine[ROWS:].astype(jnp.bfloat16)
                 else:
-                    start = (2 + (part - 2) % 3) * ROWS
-                    here = upper if part < 4 else jnp.logical_not(upper)
-                    term = jnp.where(here, s_result[start : start + ROWS], 0.0)
-                target[:ROWS, lanes] = (mine[:ROWS] + term).astype(jnp.bfloat16)
-                target[ROWS:, lanes] = mine[ROWS:].astype(jnp.bfloat16)
-            else:
-                target[:, lanes] = mine.astype(jnp.bfloat16)
-
-
-def experts(place, group, matrices, pieces, weights, shared):
+                    target[:, lanes] = mine.astype(jnp.bfloat16)
+
+
+def experts(place, matrices, pieces, weights, shared):
     width = pieces[0].shape[1]
     hbm, vmem = whole(pl.ANY), whole()
     scratch = [
-        pltpu.VMEM((GROUP_ROWS, width), jnp.bfloat16),
-        pltpu.VMEM((2 * SLOTS, width), jnp.bfloat16),
-        pltpu.VMEM((SLOTS, FF_E), jnp.bfloat16),
+        pltpu.VMEM((2 * GROUP_ROWS, width), jnp.bfloat16),
+        pltpu.VMEM((4 * SLOTS, width), jnp.bfloat16),
+        pltpu.VMEM((2 * SLOTS, FF_E), jnp.bfloat16),
         pltpu.VMEM((DEPTH, width, CHUNK), jnp.bfloat16),
         pltpu.VMEM((DEPTH, width, CHUNK), jnp.bfloat16),
         pltpu.VMEM((2, FF_E, width), jnp.bfloat16),
-        pltpu.SemaphoreType.DMA((PIECES,)),
+        pltpu.SemaphoreType.DMA((2 * PIECES,)),
         pltpu.SemaphoreType.DMA((DEPTH, 2)),
         pltpu.SemaphoreType.DMA((2,)),
+        *[pltpu.VMEM(array.shape, array.dtype) for array in shared],
+        pltpu.SemaphoreType.DMA((3,)),
+        pltpu.VMEM((BLOCK, width), jnp.bfloat16),
+        pltpu.VMEM((BLOCK, shared[2].shape[0]), jnp.bfloat16),
     ]
-    operands = [place, *matrices, *pieces, *weights]
-    if shared is not None:
-        operands += list(shared)
-        scratch += [pltpu.VMEM(array.shape, array.dtype) for array in shared]
-        scratch += [
-            pltpu.SemaphoreType.DMA((3,)),
-            pltpu.VMEM((BLOCK, width), jnp.bfloat16),
-            pltpu.VMEM((BLOCK, shared[2].shape[0]), jnp.bfloat16),
-        ]
+    operands = [place, *matrices, *pieces, *weights, *shared]
     in_specs = [whole(pltpu.SMEM)] + [vmem] * 3
     in_specs += [hbm] * (len(operands) - len(in_specs))
     return pl.pallas_call(
-        lambda *refs: experts_kernel(group, shared is not None, *refs),
-        out_shape=(jax.ShapeDtypeStruct((PIECE, width), jnp.bfloat16),) * PIECES,
+        experts_kernel,
+        out_shape=(jax.ShapeDtypeStruct((PIECE, width), jnp.bfloat16),) * (2 * PIECES),
         in_specs=in_specs,
-        out_specs=(vmem,) * PIECES,
+        out_specs=(vmem,) * (2 * PIECES),
         scratch_shapes=scratch,
-        compiler_params=pltpu.CompilerParams(vmem_limit_bytes=SCOPED[shared is not None] * 2**20),
+        compiler_params=pltpu.CompilerParams(vmem_limit_bytes=60 * 2**20),
         cost_estimate=pl.CostEstimate(
-            flops=10**10, bytes_accessed=44 * 10**6, transcendentals=10**6
+            flops=2 * 10**10, bytes_accessed=60 * 10**6, transcendentals=2 * 10**6
         ),
     )(*operands)
-
-
-SCOPED = {True: 50, False: 40}
 
 
 def gather_plane(rows):
@@ -645,24 +630,30 @@
     )
 
 
-def routing_tables(expert_ids, route_weight, place):
-    count = expert_ids.shape[1]
+def routing_slices(expert_ids, route_weight):
     packed = jnp.concatenate([expert_ids.T.astype(jnp.float32), route_weight.T], axis=0)
-    pair = jnp.stack([packed, send(packed, X_SWAP)])
-    steps = [pair, send(pair, Z_ON), send(pair, Z_TWO), send(pair, Z_BACK)]
-    slices = jnp.stack(steps).reshape(NZ, 2, 2 * count, 4, ROWS).transpose(0, 1, 3, 2, 4)
-    slices = slices.reshape(-1, 2 * count, ROWS)
-    order = lax.dynamic_index_in_dim(jnp.asarray(slice_order()), place[1], 0, keepdims=False)
-    listed = slices[order.reshape(-1)].reshape(2, 16, 2 * count, ROWS)
-    first_expert = 2 * (place[0] * 4 + place[1])
-    local = (first_expert + lax.iota(jnp.int32, 2)).astype(jnp.float32)
-    match = listed[:, None, :, :count] == local[None, :, None, None, None]
-    hit = jnp.any(match, axis=3).reshape(2, 2, GROUP_ROWS)
-    weight = jnp.sum(jnp.where(match, listed[:, None, :, count:], 0.0), axis=3)
-    weight = weight.reshape(2, 2, GROUP_ROWS)
-    ones = hit.astype(jnp.int32)
-    slot = jnp.where(hit, jnp.cumsum(ones, axis=2) - 1, -1)
-    return routing_matrices(slot.reshape(4, GROUP_ROWS), weight.reshape(4, GROUP_ROWS))
+    packed = packed.reshape(-1, 4, ROWS).transpose(1, 0, 2)
+    blocks = 2 * NZ
+    slices = lax.all_to_all(
+        jnp.broadcast_to(packed[None], (blocks, *packed.shape)), "tok", split_axis=0, concat_axis=0, tiled=True
+    ).reshape(-1, *packed.shape[1:])
+    return slices
+
+
+def routing_tables(slices, place, device):
+    order = lax.dynamic_index_in_dim(jnp.asarray(slice_order()), device, 0, keepdims=False)
+    return pl.pallas_call(
+        routing_kernel,
+        out_shape=(
+            jax.ShapeDtypeStruct((2, 2 * SLOTS, GROUP_ROWS), jnp.bfloat16),
+            jax.ShapeDtypeStruct((2, GROUP_ROWS, 2 * SLOTS), jnp.bfloat16),
+            jax.ShapeDtypeStruct((2, 2 * SLOTS, 1), jnp.float32),
+        ),
+        in_specs=[whole(pltpu.SMEM), whole(pltpu.SMEM), whole()],
+        out_specs=(whole(),) * 3,
+        scratch_shapes=[pltpu.VMEM((slices.shape[1], 2 * GROUP_ROWS), jnp.float32)],
+        compiler_params=pltpu.CompilerParams(vmem_limit_bytes=24 * 2**20),
+    )(place, order, slices)
 
 
 def block_pairs(target):
@@ -706,17 +697,16 @@
     near_x = move(own_later, lambda z, x: (z, 1) if x == 0 else None)
     weights = (expert_gate, expert_up, expert_down)
     shared = (shared_gate.T, shared_up.T, shared_down)
-    touched = touch((*weights, *shared), own)
-    near_z, touched = lax.optimization_barrier((near_z, touched))
+    near_z, slices = lax.optimization_barrier((near_z, routing_slices(expert_ids, route_weight)))
     cross = move(near_z, lambda z, x: (z, 1 - x))
     far = move(near_z, lambda z, x: (z + 1, x))
     far_cross = move(near_z, lambda z, x: (z + 1, 0) if x == 1 else None)
 
-    tables = routing_tables(expert_ids, route_weight, place)
+    tables = routing_tables(slices, place, tok_here * 4 + hd_here)
     query_segment = lax.dynamic_slice_in_dim(segment_ids, tok_here * BLOCK, BLOCK, 0)[:, None]
+    queries, tables = lax.optimization_barrier((queries, tables))
     sent, kept = attention(
-        place, segment_ids, query_segment, queries, own, near_x, near_z, cross, far, far_cross, out_proj,
-        (touched, touched),
+        place, segment_ids, query_segment, queries, own, near_x, near_z, cross, far, far_cross, out_proj
     )
     kept = kept + send(sent, CORE_SWAP).astype(jnp.float32)
     resid_rows = (
@@ -729,11 +719,11 @@
     steps = [normed]
     for _ in range(3):
         steps.append(send(steps[-1], Z_ON))
-    sums = []
+    pieces = []
     for group in range(2):
-        gathered = gather_plane(jnp.concatenate(steps[2 * group : 2 * group + 2], axis=0))
-        terms = experts(place, group, tables, gathered, weights, shared if group == 0 else None)
-        sums.append(sum_plane(*terms))
+        pieces += gather_plane(jnp.concatenate(steps[2 * group : 2 * group + 2], axis=0))
+    terms = experts(place, tables, pieces, weights, shared)
+    sums = [sum_plane(*terms[group * PIECES : (group + 1) * PIECES]) for group in range(2)]
     returned = [
         send(part.astype(jnp.bfloat16), pairs).astype(jnp.float32)
         for part, pairs in ((sums[0][ROWS:], Z_BACK), (sums[1][:ROWS], Z_TWO), (sums[1][ROWS:], Z_ON))

time: 250 us -> 230 us (0.920)
  Pallas kernels: 70.4 us -> 50.8 us
  starting transfers between devices: 67.9 us -> 49.2 us
  waiting for transfers between devices: 92.5 us -> 109 us
    ppermute x42 -> x38, waiting for transfers between devices: 74.3 us -> 104 us  [send(): return lax.ppermute(array, BOTH, pairs)]
    ppermute x42 -> x38, starting transfers between devices: 51.2 us -> 25.1 us  [send(): return lax.ppermute(array, BOTH, pairs)]
    pallas_call x4 -> x2, Pallas kernels: 59.4 us -> 40 us  [the longest x1 37.5 us: experts(): pl.pallas_call(experts_kernel, out_shape=(jax.ShapeDtypeStruct((PIECE, wi...]
    ppermute x5, waiting for transfers between devices: 18.2 us -> 5.13 us  [move(): return lax.ppermute(array, 'tok', block_pairs(target))]
    all_to_all x0 -> x1, starting transfers between devices: none -> 4 us  [routing_slices(): lax.all_to_all(jnp.broadcast_to(packed[None], (blocks, *packed.shape)), '...]
    ppermute x5, starting transfers between devices: 16.8 us -> 20.2 us  [move(): return lax.ppermute(array, 'tok', block_pairs(target))]
    unnamed x34 -> x68, local copies, waits for them, and re-layouts: 3.85 us -> 6.96 us
  transfers between devices with their start and end apart: 47 -> 44, of which waited for: 15 -> 22; matrix products, arithmetic and copies ran while one was open for 4% -> 4% of each run, Pallas kernels for 25% -> 3%
where the time goes in v2:
time: 230 us
  waiting for transfers between devices  109 us (47%)
  Pallas kernels  50.8 us (22%)
  starting transfers between devices  49.2 us (21%)
  local copies, waits for them, and re-layouts  9.99 us (4%)
  other arithmetic  8.97 us (4%)
    ppermute x38, waiting for transfers between devices, send(): return lax.ppermute(array, BOTH, pairs)  104 us
    pallas_call x1, Pallas kernels, experts(): pl.pallas_call(experts_kernel, out_shape=(jax.ShapeDtypeStruct((PIECE, wi...  37.5 us
    ppermute x38, starting transfers between devices, send(): return lax.ppermute(array, BOTH, pairs)  25.1 us
    ppermute x5, starting transfers between devices, move(): return lax.ppermute(array, 'tok', block_pairs(target))  20.2 us
    unnamed x68, local copies, waits for them, and re-layouts  6.96 us
    pallas_call x1, Pallas kernels, attention(): pl.pallas_call(attention_second, out_shape=(jax.ShapeDtypeStruct((2 * ROW...  5.27 us
    ppermute x5, waiting for transfers between devices, move(): return lax.ppermute(array, 'tok', block_pairs(target))  5.13 us
  transfers between devices with their start and end apart: 44, of which 22 were waited for; matrix products, arithmetic and copies ran while one was open for 4% of the time, Pallas kernels for 3%

profile of v2, /device:TPU:0, one launch (start us, length us, event | category | flops | bytes accessed | tf_op | source)
XLA Modules:
  0.0 229.7 jit_solution(14919294747033961474)
XLA Ops:
  3.5 5.7 %collective-permute-start = (bf16[256,1024]{1,0:T(8,128)(2,1)}, bf16[256,1024]{1,0:T(8,128)(2,1)}, u32[]{:S(2)}, u32[]{:S(2)}) collective-permute-start(bf16[256,1024]{1,0:T(8,128)(2,1)} %get-tuple-element.42.own), channel_id=1, source_target_pairs={{0,8},{4,12},{8,16},{12,20},{16,24},{20,28},{1,9},{5,13},{9,17},{1... | collective-permute-start | bytes 1572872 | tf_op jit(solution)/shard_map/ppermute | solution.py:693
  11.5 4.0 %all-to-all-start = ((f32[8,1,3072]{2,1,0:T(1,128)}), f32[8,1,3072]{2,1,0:T(1,128)S(1)}, u32[]{:S(2)}, u32[]{:S(2)}) async-start(f32[8,1,3072]{2,1,0:T(1,128)} %reshape.26), calls=%async_computation | async-start | bytes 196608 | tf_op jit(solution)/shard_map/all_to_all | solution.py:637
  15.5 5.1 %collective-permute-done.near_z = bf16[256,1024]{1,0:T(8,128)(2,1)} collective-permute-done((bf16[256,1024]{1,0:T(8,128)(2,1)}, bf16[256,1024]{1,0:T(8,128)(2,1)}, u32[]{:S(2)}, u32[]{:S(2)}) %collective-permute-start) | collective-permute-done | bytes 524320 | tf_op jit(solution)/shard_map/ppermute | solution.py:693
  20.7 4.2 %collective-permute-start.4 = (bf16[256,1024]{1,0:T(8,128)(2,1)}, bf16[256,1024]{1,0:T(8,128)(2,1)}, u32[]{:S(2)}, u32[]{:S(2)}) collective-permute-start(bf16[256,1024]{1,0:T(8,128)(2,1)} %get-tuple-element.42.own), channel_id=1, source_target_pairs={{0,4},{8,12},{16,20},{24,28},{1,5},{9,13},{17,21},{25,29},{2,6},{1... | collective-permute-start | bytes 1572872 | tf_op jit(solution)/shard_map/ppermute | solution.py:693
  27.1 5.0 %collective-permute-start.2 = (bf16[256,1024]{1,0:T(8,128)(2,1)}, bf16[256,1024]{1,0:T(8,128)(2,1)S(1)}, u32[]{:S(2)}, u32[]{:S(2)}) collective-permute-start(bf16[256,1024]{1,0:T(8,128)(2,1)} %collective-permute-done.near_z), channel_id=1, source_target_pairs={{0,8},{4,12},{8,16},{12,20},{16,24},{20,28},{1,9},{5,13},{9,17},{1... | collective-permute-start | bytes 1572872 | tf_op jit(solution)/shard_map/ppermute | solution.py:693
  32.2 4.5 %collective-permute-start.1 = (bf16[256,1024]{1,0:T(8,128)(2,1)}, bf16[256,1024]{1,0:T(8,128)(2,1)}, u32[]{:S(2)}, u32[]{:S(2)}) collective-permute-start(bf16[256,1024]{1,0:T(8,128)(2,1)} %collective-permute-done.near_z), channel_id=1, source_target_pairs={{0,4},{4,0},{8,12},{12,8},{16,20},{20,16},{24,28},{28,24},{1,5},{5... | collective-permute-start | bytes 1572872 | tf_op jit(solution)/shard_map/ppermute | solution.py:693
  46.7 3.3 %shard_map.178 = (f32[256,4]{1,0:T(8,128)S(1)}, f32[256,4]{1,0:T(8,128)S(1)}, f32[4,256,128]{2,1,0:T(8,128)S(1)}) custom-call(s32[2]{0:T(128)S(1)} %copy-done.2, s32[8,256]{1,0:T(8,128)S(1)} %reshape.23.segments, s32[256,1]{1,0:T(8,128)S(1)} %copy.25.query_segment, bf16[256,512]{1,0:T(8,128)(2,1)S(1)} %copy-done.1, bf16[256,1024]{1,0:T(8,128)(2,1)S(1)} %copy-done.5, ...), custom_call_target="tpu_custom_call" | custom-call | flops 800000000 | bytes 4000000 | tf_op jit(solution)/shard_map/pallas_call | solution.py:374
  50.0 5.3 %shard_map.179 = (bf16[128,2048]{1,0:T(8,128)(2,1)S(1)}, f32[128,2048]{1,0:T(8,128)S(1)}) custom-call(s32[2]{0:T(128)S(1)} %copy-done.2, s32[8,256]{1,0:T(8,128)S(1)} %reshape.23.segments, s32[256,1]{1,0:T(8,128)S(1)} %copy.25.query_segment, bf16[256,512]{1,0:T(8,128)(2,1)S(1)} %copy-done.1, bf16[256,1024]{1,0:T(8,128)(2,1)} %collective-permute-done.1.cross, ...), custom_call_target="tpu_custom_call" | custom-call | flops 1000000000 | bytes 6000000 | tf_op jit(solution)/shard_map/pallas_call | solution.py:382
  59.1 6.8 %collective-permute-done.6 = bf16[64,2048]{1,0:T(8,128)(2,1)S(1)} collective-permute-done((bf16[64,2048]{1,0:T(8,128)(2,1)S(1)}, bf16[64,2048]{1,0:T(8,128)(2,1)S(1)}, u32[]{:S(2)}, u32[]{:S(2)}) %collective-permute-start.6) | collective-permute-done | bytes 262176 | tf_op jit(solution)/shard_map/ppermute | solution.py:244
  67.2 5.0 %collective-permute-start.7 = (bf16[64,2048]{1,0:T(8,128)(2,1)S(1)}, bf16[64,2048]{1,0:T(8,128)(2,1)S(1)}, u32[]{:S(2)}, u32[]{:S(2)}) collective-permute-start(bf16[64,2048]{1,0:T(8,128)(2,1)S(1)} %multiply_convert_fusion), channel_id=1, source_target_pairs={{0,8},{1,9},{2,10},{3,11},{4,12},{5,13},{6,14},{7,15},{8,24},{9,25... | collective-permute-start | bytes 786440 | tf_op jit(solution)/shard_map/ppermute | solution.py:244
  72.2 6.9 %collective-permute-done.7 = bf16[64,2048]{1,0:T(8,128)(2,1)S(1)} collective-permute-done((bf16[64,2048]{1,0:T(8,128)(2,1)S(1)}, bf16[64,2048]{1,0:T(8,128)(2,1)S(1)}, u32[]{:S(2)}, u32[]{:S(2)}) %collective-permute-start.7) | collective-permute-done | bytes 262176 | tf_op jit(solution)/shard_map/ppermute | solution.py:244
  79.7 7.2 %collective-permute-done.15 = bf16[64,2048]{1,0:T(8,128)(2,1)S(1)} collective-permute-done((bf16[64,2048]{1,0:T(8,128)(2,1)S(1)}, bf16[64,2048]{1,0:T(8,128)(2,1)S(1)}, u32[]{:S(2)}, u32[]{:S(2)}) %collective-permute-start.15) | collective-permute-done | bytes 262176 | tf_op jit(solution)/shard_map/ppermute | solution.py:244
  88.0 6.2 %collective-permute-done.16 = bf16[64,2048]{1,0:T(8,128)(2,1)S(1)} collective-permute-done((bf16[64,2048]{1,0:T(8,128)(2,1)S(1)}, bf16[64,2048]{1,0:T(8,128)(2,1)S(1)}, u32[]{:S(2)}, u32[]{:S(2)}) %collective-permute-start.16) | collective-permute-done | bytes 262176 | tf_op jit(solution)/shard_map/ppermute | solution.py:244
  98.7 8.5 %collective-permute-done.18.refs_14_ = bf16[128,2048]{1,0:T(8,128)(2,1)S(1)} collective-permute-done((bf16[128,2048]{1,0:T(8,128)(2,1)S(1)}, bf16[128,2048]{1,0:T(8,128)(2,1)S(1)}, u32[]{:S(2)}, u32[]{:S(2)}) %collective-permute-start.18) | collective-permute-done | bytes 524320 | tf_op jit(solution)/shard_map/ppermute | solution.py:244
  111.3 7.1 %collective-permute-done.10.refs_7_ = bf16[128,2048]{1,0:T(8,128)(2,1)S(1)} collective-permute-done((bf16[128,2048]{1,0:T(8,128)(2,1)S(1)}, bf16[128,2048]{1,0:T(8,128)(2,1)S(1)}, u32[]{:S(2)}, u32[]{:S(2)}) %collective-permute-start.10) | collective-permute-done | bytes 524320 | tf_op jit(solution)/shard_map/ppermute | solution.py:244
  118.5 4.0 %collective-permute-done.20.refs_16_ = bf16[128,2048]{1,0:T(8,128)(2,1)S(1)} collective-permute-done((bf16[128,2048]{1,0:T(8,128)(2,1)S(1)}, bf16[128,2048]{1,0:T(8,128)(2,1)S(1)}, u32[]{:S(2)}, u32[]{:S(2)}) %collective-permute-start.20) | collective-permute-done | bytes 524320 | tf_op jit(solution)/shard_map/ppermute | solution.py:244
  122.5 3.5 %collective-permute-done.19.refs_15_ = bf16[128,2048]{1,0:T(8,128)(2,1)S(1)} collective-permute-done((bf16[128,2048]{1,0:T(8,128)(2,1)S(1)}, bf16[128,2048]{1,0:T(8,128)(2,1)S(1)}, u32[]{:S(2)}, u32[]{:S(2)}) %collective-permute-start.19) | collective-permute-done | bytes 524320 | tf_op jit(solution)/shard_map/ppermute | solution.py:244
  128.7 37.5 %shard_map.180 = (bf16[128,2048]{1,0:T(8,128)(2,1)}, bf16[128,2048]{1,0:T(8,128)(2,1)}, bf16[128,2048]{1,0:T(8,128)(2,1)}, bf16[128,2048]{1,0:T(8,128)(2,1)}, bf...) custom-call(s32[2]{0:T(128)} %pad_add_fusion.place.refs_0_, ...), custom_call_target="tpu_custom_call" | custom-call | flops 20000000000 | bytes 60000000 | tf_op jit(solution)/shard_map/pallas_call | solution.py:596
  174.6 8.0 %collective-permute-done.26 = bf16[128,2048]{1,0:T(8,128)(2,1)S(1)} collective-permute-done((bf16[128,2048]{1,0:T(8,128)(2,1)S(1)}, bf16[128,2048]{1,0:T(8,128)(2,1)S(1)}, u32[]{:S(2)}, u32[]{:S(2)}) %collective-permute-start.26) | collective-permute-done | bytes 524320 | tf_op jit(solution)/shard_map/ppermute | solution.py:244
  185.6 9.8 %collective-permute-done.39 = bf16[128,2048]{1,0:T(8,128)(2,1)S(1)} collective-permute-done((bf16[128,2048]{1,0:T(8,128)(2,1)S(1)}, bf16[128,2048]{1,0:T(8,128)(2,1)S(1)}, u32[]{:S(2)}, u32[]{:S(2)}) %collective-permute-start.39) | collective-permute-done | bytes 524320 | tf_op jit(solution)/shard_map/ppermute | solution.py:244
  197.5 4.0 %collective-permute-done.31 = bf16[128,2048]{1,0:T(8,128)(2,1)S(1)} collective-permute-done((bf16[128,2048]{1,0:T(8,128)(2,1)S(1)}, bf16[128,2048]{1,0:T(8,128)(2,1)S(1)}, u32[]{:S(2)}, u32[]{:S(2)}) %collective-permute-start.31) | collective-permute-done | bytes 524320 | tf_op jit(solution)/shard_map/ppermute | solution.py:244
  203.2 3.9 %collective-permute-done.40 = bf16[128,2048]{1,0:T(8,128)(2,1)S(1)} collective-permute-done((bf16[128,2048]{1,0:T(8,128)(2,1)S(1)}, bf16[128,2048]{1,0:T(8,128)(2,1)S(1)}, u32[]{:S(2)}, u32[]{:S(2)}) %collective-permute-start.40) | collective-permute-done | bytes 524320 | tf_op jit(solution)/shard_map/ppermute | solution.py:244
  210.7 7.9 %collective-permute-done.41 = bf16[64,2048]{1,0:T(8,128)(2,1)S(1)} collective-permute-done((bf16[64,2048]{1,0:T(8,128)(2,1)S(1)}, bf16[64,2048]{1,0:T(8,128)(2,1)S(1)}, u32[]{:S(2)}, u32[]{:S(2)}) %collective-permute-start.41) | collective-permute-done | bytes 262176 | tf_op jit(solution)/shard_map/ppermute | solution.py:244
  218.6 10.3 %collective-permute-done.42 = bf16[64,2048]{1,0:T(8,128)(2,1)S(1)} collective-permute-done((bf16[64,2048]{1,0:T(8,128)(2,1)S(1)}, bf16[64,2048]{1,0:T(8,128)(2,1)S(1)}, u32[]{:S(2)}, u32[]{:S(2)}) %collective-permute-start.42) | collective-permute-done | bytes 262176 | tf_op jit(solution)/shard_map/ppermute | solution.py:244
  (166 shorter events, 54.7 us)
Async XLA Ops:
  3.5 17.2 %collective-permute-start = (bf16[256,1024]{1,0:T(8,128)(2,1)}, bf16[256,1024]{1,0:T(8,128)(2,1)}, u32[]{:S(2)}, u32[]{:S(2)}) collective-permute-start(bf16[256,1024]{1,0:T(8,128)(2,1)} %get-tuple-element.42.own), channel_id=1, source_target_pairs={{0,8},{4,12},{8,16},{12,20},{16,24},{20,28},{1,9},{5,13},{9,17},{1... | collective-permute-start | bytes 1572872 | tf_op jit(solution)/shard_map/ppermute | solution.py:693
  11.5 13.3 %all-to-all-start = ((f32[8,1,3072]{2,1,0:T(1,128)}), f32[8,1,3072]{2,1,0:T(1,128)S(1)}, u32[]{:S(2)}, u32[]{:S(2)}) async-start(f32[8,1,3072]{2,1,0:T(1,128)} %reshape.26), calls=%async_computation | async-start | bytes 196608 | tf_op jit(solution)/shard_map/all_to_all | solution.py:637
  20.7 23.9 %collective-permute-start.4 = (bf16[256,1024]{1,0:T(8,128)(2,1)}, bf16[256,1024]{1,0:T(8,128)(2,1)}, u32[]{:S(2)}, u32[]{:S(2)}) collective-permute-start(bf16[256,1024]{1,0:T(8,128)(2,1)} %get-tuple-element.42.own), channel_id=1, source_target_pairs={{0,4},{8,12},{16,20},{24,28},{1,5},{9,13},{17,21},{25,29},{2,6},{1... | collective-permute-start | bytes 1572872 | tf_op jit(solution)/shard_map/ppermute | solution.py:693
  26.4 23.6 %collective-permute-start.3 = (bf16[256,1024]{1,0:T(8,128)(2,1)}, bf16[256,1024]{1,0:T(8,128)(2,1)S(1)}, u32[]{:S(2)}, u32[]{:S(2)}) collective-permute-start(bf16[256,1024]{1,0:T(8,128)(2,1)} %collective-permute-done.near_z), channel_id=1, source_target_pairs={{4,8},{12,16},{20,24},{5,9},{13,17},{21,25},{6,10},{14,18},{22,26}... | collective-permute-start | bytes 1572872 | tf_op jit(solution)/shard_map/ppermute | solution.py:693
  27.1 22.9 %collective-permute-start.2 = (bf16[256,1024]{1,0:T(8,128)(2,1)}, bf16[256,1024]{1,0:T(8,128)(2,1)S(1)}, u32[]{:S(2)}, u32[]{:S(2)}) collective-permute-start(bf16[256,1024]{1,0:T(8,128)(2,1)} %collective-permute-done.near_z), channel_id=1, source_target_pairs={{0,8},{4,12},{8,16},{12,20},{16,24},{20,28},{1,9},{5,13},{9,17},{1... | collective-permute-start | bytes 1572872 | tf_op jit(solution)/shard_map/ppermute | solution.py:693
  32.2 17.8 %collective-permute-start.1 = (bf16[256,1024]{1,0:T(8,128)(2,1)}, bf16[256,1024]{1,0:T(8,128)(2,1)}, u32[]{:S(2)}, u32[]{:S(2)}) collective-permute-start(bf16[256,1024]{1,0:T(8,128)(2,1)} %collective-permute-done.near_z), channel_id=1, source_target_pairs={{0,4},{4,0},{8,12},{12,8},{16,20},{20,16},{24,28},{28,24},{1,5},{5... | collective-permute-start | bytes 1572872 | tf_op jit(solution)/shard_map/ppermute | solution.py:693
  94.2 13.0 %collective-permute-start.18 = (bf16[128,2048]{1,0:T(8,128)(2,1)S(1)}, bf16[128,2048]{1,0:T(8,128)(2,1)S(1)}, u32[]{:S(2)}, u32[]{:S(2)}) collective-permute-start(bf16[128,2048]{1,0:T(8,128)(2,1)S(1)} %constant_dynamic-update-slice_fusion.refs_12_), channel_id=1, source_target_pairs={{0,4},{1,3},{2,6},{3,1},{4,0},{5,7},{6,2},{7,5},{8,12},{9,11},{10,... | collective-permute-start | bytes 1572872 | tf_op jit(solution)/shard_map/ppermute | solution.py:244
  94.8 14.0 %collective-permute-start.17 = (bf16[128,2048]{1,0:T(8,128)(2,1)S(1)}, bf16[128,2048]{1,0:T(8,128)(2,1)S(1)}, u32[]{:S(2)}, u32[]{:S(2)}) collective-permute-start(bf16[128,2048]{1,0:T(8,128)(2,1)S(1)} %constant_dynamic-update-slice_fusion.refs_12_), channel_id=1, source_target_pairs={{0,1},{1,0},{2,3},{3,2},{4,5},{5,4},{6,7},{7,6},{8,9},{9,8},{10,11... | collective-permute-start | bytes 1572872 | tf_op jit(solution)/shard_map/ppermute | solution.py:244
  96.5 12.6 %collective-permute-start.12 = (bf16[128,2048]{1,0:T(8,128)(2,1)S(1)}, bf16[128,2048]{1,0:T(8,128)(2,1)S(1)}, u32[]{:S(2)}, u32[]{:S(2)}) collective-permute-start(bf16[128,2048]{1,0:T(8,128)(2,1)S(1)} %collective-permute-done.9.refs_6_), channel_id=1, source_target_pairs={{0,1},{1,0},{2,3},{3,2},{4,5},{5,4},{6,7},{7,6},{8,9},{9,8},{10,11... | collective-permute-start | bytes 1572872 | tf_op jit(solution)/shard_map/ppermute | solution.py:244
  96.5 14.8 %collective-permute-start.11 = (bf16[128,2048]{1,0:T(8,128)(2,1)S(1)}, bf16[128,2048]{1,0:T(8,128)(2,1)S(1)}, u32[]{:S(2)}, u32[]{:S(2)}) collective-permute-start(bf16[128,2048]{1,0:T(8,128)(2,1)S(1)} %collective-permute-done.9.refs_6_), channel_id=1, source_target_pairs={{0,2},{1,5},{2,0},{3,7},{4,6},{5,1},{6,4},{7,3},{8,10},{9,13},{10,... | collective-permute-start | bytes 1572872 | tf_op jit(solution)/shard_map/ppermute | solution.py:244
  98.0 20.4 %collective-permute-start.10 = (bf16[128,2048]{1,0:T(8,128)(2,1)S(1)}, bf16[128,2048]{1,0:T(8,128)(2,1)S(1)}, u32[]{:S(2)}, u32[]{:S(2)}) collective-permute-start(bf16[128,2048]{1,0:T(8,128)(2,1)S(1)} %collective-permute-done.8.refs_5_), channel_id=1, source_target_pairs={{0,4},{1,3},{2,6},{3,1},{4,0},{5,7},{6,2},{7,5},{8,12},{9,11},{10,... | collective-permute-start | bytes 1572872 | tf_op jit(solution)/shard_map/ppermute | solution.py:244
  107.2 15.2 %collective-permute-start.20 = (bf16[128,2048]{1,0:T(8,128)(2,1)S(1)}, bf16[128,2048]{1,0:T(8,128)(2,1)S(1)}, u32[]{:S(2)}, u32[]{:S(2)}) collective-permute-start(bf16[128,2048]{1,0:T(8,128)(2,1)S(1)} %collective-permute-done.18.refs_14_), channel_id=1, source_target_pairs={{0,2},{1,5},{2,0},{3,7},{4,6},{5,1},{6,4},{7,3},{8,10},{9,13},{10,... | collective-permute-start | bytes 1572872 | tf_op jit(solution)/shard_map/ppermute | solution.py:244
  108.7 17.2 %collective-permute-start.19 = (bf16[128,2048]{1,0:T(8,128)(2,1)S(1)}, bf16[128,2048]{1,0:T(8,128)(2,1)S(1)}, u32[]{:S(2)}, u32[]{:S(2)}) collective-permute-start(bf16[128,2048]{1,0:T(8,128)(2,1)S(1)} %collective-permute-done.17.refs_13_), channel_id=1, source_target_pairs={{0,4},{1,3},{2,6},{3,1},{4,0},{5,7},{6,2},{7,5},{8,12},{9,11},{10,... | collective-permute-start | bytes 1572872 | tf_op jit(solution)/shard_map/ppermute | solution.py:244
  109.1 16.8 %collective-permute-start.21 = (bf16[128,2048]{1,0:T(8,128)(2,1)S(1)}, bf16[128,2048]{1,0:T(8,128)(2,1)S(1)}, u32[]{:S(2)}, u32[]{:S(2)}) collective-permute-start(bf16[128,2048]{1,0:T(8,128)(2,1)S(1)} %collective-permute-done.18.refs_14_), channel_id=1, source_target_pairs={{0,1},{1,0},{2,3},{3,2},{4,5},{5,4},{6,7},{7,6},{8,9},{9,8},{10,11... | collective-permute-start | bytes 1572872 | tf_op jit(solution)/shard_map/ppermute | solution.py:244
  111.3 14.6 %collective-permute-start.14 = (bf16[128,2048]{1,0:T(8,128)(2,1)S(1)}, bf16[128,2048]{1,0:T(8,128)(2,1)S(1)}, u32[]{:S(2)}, u32[]{:S(2)}) collective-permute-start(bf16[128,2048]{1,0:T(8,128)(2,1)S(1)} %collective-permute-done.11.refs_8_), channel_id=1, source_target_pairs={{0,1},{1,0},{2,3},{3,2},{4,5},{5,4},{6,7},{7,6},{8,9},{9,8},{10,11... | collective-permute-start | bytes 1572872 | tf_op jit(solution)/shard_map/ppermute | solution.py:244
  167.2 17.7 %collective-permute-start.37 = (bf16[128,2048]{1,0:T(8,128)(2,1)}, bf16[128,2048]{1,0:T(8,128)(2,1)S(1)}, u32[]{:S(2)}, u32[]{:S(2)}) collective-permute-start(bf16[128,2048]{1,0:T(8,128)(2,1)} %get-tuple-element.64), channel_id=1, source_target_pairs={{0,1},{1,0},{2,3},{3,2},{4,5},{5,4},{6,7},{7,6},{8,9},{9,8},{10,11... | collective-permute-start | bytes 1572872 | tf_op jit(solution)/shard_map/ppermute | solution.py:244
  169.8 12.9 %collective-permute-start.26 = (bf16[128,2048]{1,0:T(8,128)(2,1)S(1)}, bf16[128,2048]{1,0:T(8,128)(2,1)S(1)}, u32[]{:S(2)}, u32[]{:S(2)}) collective-permute-start(bf16[128,2048]{1,0:T(8,128)(2,1)S(1)} %add_convert_fusion.6), channel_id=1, source_target_pairs={{0,4},{1,3},{2,6},{3,1},{4,0},{5,7},{6,2},{7,5},{8,12},{9,11},{10,... | collective-permute-start | bytes 1572872 | tf_op jit(solution)/shard_map/ppermute | solution.py:244
  172.1 12.1 %collective-permute-start.30 = (bf16[128,2048]{1,0:T(8,128)(2,1)S(1)}, bf16[128,2048]{1,0:T(8,128)(2,1)S(1)}, u32[]{:S(2)}, u32[]{:S(2)}) collective-permute-start(bf16[128,2048]{1,0:T(8,128)(2,1)S(1)} %add_convert_fusion.5), channel_id=1, source_target_pairs={{0,2},{1,5},{2,0},{3,7},{4,6},{5,1},{6,4},{7,3},{8,10},{9,13},{10,... | collective-permute-start | bytes 1572872 | tf_op jit(solution)/shard_map/ppermute | solution.py:244
  173.8 21.7 %collective-permute-start.39 = (bf16[128,2048]{1,0:T(8,128)(2,1)S(1)}, bf16[128,2048]{1,0:T(8,128)(2,1)S(1)}, u32[]{:S(2)}, u32[]{:S(2)}) collective-permute-start(bf16[128,2048]{1,0:T(8,128)(2,1)S(1)} %add_convert_fusion.2), channel_id=1, source_target_pairs={{0,2},{1,5},{2,0},{3,7},{4,6},{5,1},{6,4},{7,3},{8,10},{9,13},{10,... | collective-permute-start | bytes 1572872 | tf_op jit(solution)/shard_map/ppermute | solution.py:244
  174.5 21.2 %collective-permute-start.24 = (bf16[128,2048]{1,0:T(8,128)(2,1)S(1)}, bf16[128,2048]{1,0:T(8,128)(2,1)S(1)}, u32[]{:S(2)}, u32[]{:S(2)}) collective-permute-start(bf16[128,2048]{1,0:T(8,128)(2,1)S(1)} %copy-done.17), channel_id=1, source_target_pairs={{0,1},{1,0},{2,3},{3,2},{4,5},{5,4},{6,7},{7,6},{8,9},{9,8},{10,11... | collective-permute-start | bytes 1572872 | tf_op jit(solution)/shard_map/ppermute | solution.py:244
  182.6 14.1 %collective-permute-start.35 = (bf16[128,2048]{1,0:T(8,128)(2,1)S(1)}, bf16[128,2048]{1,0:T(8,128)(2,1)S(1)}, u32[]{:S(2)}, u32[]{:S(2)}) collective-permute-start(bf16[128,2048]{1,0:T(8,128)(2,1)S(1)} %add_convert_fusion.3), channel_id=1, source_target_pairs={{0,4},{1,3},{2,6},{3,1},{4,0},{5,7},{6,2},{7,5},{8,12},{9,11},{10,... | collective-permute-start | bytes 1572872 | tf_op jit(solution)/shard_map/ppermute | solution.py:244
  184.2 13.3 %collective-permute-start.27 = (bf16[128,2048]{1,0:T(8,128)(2,1)S(1)}, bf16[128,2048]{1,0:T(8,128)(2,1)S(1)}, u32[]{:S(2)}, u32[]{:S(2)}) collective-permute-start(bf16[128,2048]{1,0:T(8,128)(2,1)S(1)} %collective-permute-done.26), channel_id=1, source_target_pairs={{0,1},{1,0},{2,3},{3,2},{4,5},{5,4},{6,7},{7,6},{8,9},{9,8},{10,11... | collective-permute-start | bytes 1572872 | tf_op jit(solution)/shard_map/ppermute | solution.py:244
  185.0 16.5 %collective-permute-start.31 = (bf16[128,2048]{1,0:T(8,128)(2,1)S(1)}, bf16[128,2048]{1,0:T(8,128)(2,1)S(1)}, u32[]{:S(2)}, u32[]{:S(2)}) collective-permute-start(bf16[128,2048]{1,0:T(8,128)(2,1)S(1)} %add_convert_fusion.4), channel_id=1, source_target_pairs={{0,4},{1,3},{2,6},{3,1},{4,0},{5,7},{6,2},{7,5},{8,12},{9,11},{10,... | collective-permute-start | bytes 1572872 | tf_op jit(solution)/shard_map/ppermute | solution.py:244
  210.7 18.2 %collective-permute-start.42 = (bf16[64,2048]{1,0:T(8,128)(2,1)S(1)}, bf16[64,2048]{1,0:T(8,128)(2,1)S(1)}, u32[]{:S(2)}, u32[]{:S(2)}) collective-permute-start(bf16[64,2048]{1,0:T(8,128)(2,1)S(1)} %get-tuple-element.71), channel_id=1, source_target_pairs={{0,8},{1,9},{2,10},{3,11},{4,12},{5,13},{6,14},{7,15},{8,24},{9,25... | collective-permute-start | bytes 786440 | tf_op jit(solution)/shard_map/ppermute | solution.py:244
  (52 other events, 568.1 us)

commit v3 on v2

--- a/solution.py
+++ b/solution.py
@@ -395,11 +395,11 @@
     )
 
 
-CHUNK = 256
+CHUNK = 512
 WIDE = 512
 PIECE = 2 * ROWS
 PIECES = 8
-DEPTH = 3
+DEPTH = 2
 
 
 def silu_times(gate_val, up_val):

time: 230 us -> 228 us (level)
  no operation moved by 1% of the time
where the time goes in v3:
time: 228 us
  waiting for transfers between devices  109 us (48%)
  starting transfers between devices  49.2 us (22%)
  Pallas kernels  48.6 us (21%)
  local copies, waits for them, and re-layouts  9.99 us (4%)
  other arithmetic  8.97 us (4%)
    ppermute x38, waiting for transfers between devices, send(): return lax.ppermute(array, BOTH, pairs)  104 us
    pallas_call x1, Pallas kernels, experts(): pl.pallas_call(experts_kernel, out_shape=(jax.ShapeDtypeStruct((PIECE, wi...  35.3 us
    ppermute x38, starting transfers between devices, send(): return lax.ppermute(array, BOTH, pairs)  25 us
    ppermute x5, starting transfers between devices, move(): return lax.ppermute(array, 'tok', block_pairs(target))  20.2 us
    unnamed x68, local copies, waits for them, and re-layouts  6.96 us
    pallas_call x1, Pallas kernels, attention(): pl.pallas_call(attention_second, out_shape=(jax.ShapeDtypeStruct((2 * ROW...  5.27 us
    ppermute x5, waiting for transfers between devices, move(): return lax.ppermute(array, 'tok', block_pairs(target))  5.13 us
  transfers between devices with their start and end apart: 44, of which 22 were waited for; matrix products, arithmetic and copies ran while one was open for 4% of the time, Pallas kernels for 3%

profile of v3, /device:TPU:0, one launch (start us, length us, event | category | flops | bytes accessed | tf_op | source)
XLA Modules:
  0.0 227.5 jit_solution(15580143390040463210)
XLA Ops:
  3.5 5.7 %collective-permute-start = (bf16[256,1024]{1,0:T(8,128)(2,1)}, bf16[256,1024]{1,0:T(8,128)(2,1)}, u32[]{:S(2)}, u32[]{:S(2)}) collective-permute-start(bf16[256,1024]{1,0:T(8,128)(2,1)} %get-tuple-element.42.own), channel_id=1, source_target_pairs={{0,8},{4,12},{8,16},{12,20},{16,24},{20,28},{1,9},{5,13},{9,17},{1... | collective-permute-start | bytes 1572872 | tf_op jit(solution)/shard_map/ppermute | solution.py:693
  11.5 4.0 %all-to-all-start = ((f32[8,1,3072]{2,1,0:T(1,128)}), f32[8,1,3072]{2,1,0:T(1,128)S(1)}, u32[]{:S(2)}, u32[]{:S(2)}) async-start(f32[8,1,3072]{2,1,0:T(1,128)} %reshape.26), calls=%async_computation | async-start | bytes 196608 | tf_op jit(solution)/shard_map/all_to_all | solution.py:637
  15.5 5.1 %collective-permute-done.near_z = bf16[256,1024]{1,0:T(8,128)(2,1)} collective-permute-done((bf16[256,1024]{1,0:T(8,128)(2,1)}, bf16[256,1024]{1,0:T(8,128)(2,1)}, u32[]{:S(2)}, u32[]{:S(2)}) %collective-permute-start) | collective-permute-done | bytes 524320 | tf_op jit(solution)/shard_map/ppermute | solution.py:693
  20.7 4.2 %collective-permute-start.4 = (bf16[256,1024]{1,0:T(8,128)(2,1)}, bf16[256,1024]{1,0:T(8,128)(2,1)}, u32[]{:S(2)}, u32[]{:S(2)}) collective-permute-start(bf16[256,1024]{1,0:T(8,128)(2,1)} %get-tuple-element.42.own), channel_id=1, source_target_pairs={{0,4},{8,12},{16,20},{24,28},{1,5},{9,13},{17,21},{25,29},{2,6},{1... | collective-permute-start | bytes 1572872 | tf_op jit(solution)/shard_map/ppermute | solution.py:693
  27.1 5.0 %collective-permute-start.2 = (bf16[256,1024]{1,0:T(8,128)(2,1)}, bf16[256,1024]{1,0:T(8,128)(2,1)S(1)}, u32[]{:S(2)}, u32[]{:S(2)}) collective-permute-start(bf16[256,1024]{1,0:T(8,128)(2,1)} %collective-permute-done.near_z), channel_id=1, source_target_pairs={{0,8},{4,12},{8,16},{12,20},{16,24},{20,28},{1,9},{5,13},{9,17},{1... | collective-permute-start | bytes 1572872 | tf_op jit(solution)/shard_map/ppermute | solution.py:693
  32.2 4.5 %collective-permute-start.1 = (bf16[256,1024]{1,0:T(8,128)(2,1)}, bf16[256,1024]{1,0:T(8,128)(2,1)}, u32[]{:S(2)}, u32[]{:S(2)}) collective-permute-start(bf16[256,1024]{1,0:T(8,128)(2,1)} %collective-permute-done.near_z), channel_id=1, source_target_pairs={{0,4},{4,0},{8,12},{12,8},{16,20},{20,16},{24,28},{28,24},{1,5},{5... | collective-permute-start | bytes 1572872 | tf_op jit(solution)/shard_map/ppermute | solution.py:693
  46.7 3.3 %shard_map.178 = (f32[256,4]{1,0:T(8,128)S(1)}, f32[256,4]{1,0:T(8,128)S(1)}, f32[4,256,128]{2,1,0:T(8,128)S(1)}) custom-call(s32[2]{0:T(128)S(1)} %copy-done.2, s32[8,256]{1,0:T(8,128)S(1)} %reshape.23.segments, s32[256,1]{1,0:T(8,128)S(1)} %copy.25.query_segment, bf16[256,512]{1,0:T(8,128)(2,1)S(1)} %copy-done.1, bf16[256,1024]{1,0:T(8,128)(2,1)S(1)} %copy-done.5, ...), custom_call_target="tpu_custom_call" | custom-call | flops 800000000 | bytes 4000000 | tf_op jit(solution)/shard_map/pallas_call | solution.py:374
  50.0 5.3 %shard_map.179 = (bf16[128,2048]{1,0:T(8,128)(2,1)S(1)}, f32[128,2048]{1,0:T(8,128)S(1)}) custom-call(s32[2]{0:T(128)S(1)} %copy-done.2, s32[8,256]{1,0:T(8,128)S(1)} %reshape.23.segments, s32[256,1]{1,0:T(8,128)S(1)} %copy.25.query_segment, bf16[256,512]{1,0:T(8,128)(2,1)S(1)} %copy-done.1, bf16[256,1024]{1,0:T(8,128)(2,1)} %collective-permute-done.1.cross, ...), custom_call_target="tpu_custom_call" | custom-call | flops 1000000000 | bytes 6000000 | tf_op jit(solution)/shard_map/pallas_call | solution.py:382
  59.1 6.8 %collective-permute-done.6 = bf16[64,2048]{1,0:T(8,128)(2,1)S(1)} collective-permute-done((bf16[64,2048]{1,0:T(8,128)(2,1)S(1)}, bf16[64,2048]{1,0:T(8,128)(2,1)S(1)}, u32[]{:S(2)}, u32[]{:S(2)}) %collective-permute-start.6) | collective-permute-done | bytes 262176 | tf_op jit(solution)/shard_map/ppermute | solution.py:244
  67.2 5.0 %collective-permute-start.7 = (bf16[64,2048]{1,0:T(8,128)(2,1)S(1)}, bf16[64,2048]{1,0:T(8,128)(2,1)S(1)}, u32[]{:S(2)}, u32[]{:S(2)}) collective-permute-start(bf16[64,2048]{1,0:T(8,128)(2,1)S(1)} %multiply_convert_fusion), channel_id=1, source_target_pairs={{0,8},{1,9},{2,10},{3,11},{4,12},{5,13},{6,14},{7,15},{8,24},{9,25... | collective-permute-start | bytes 786440 | tf_op jit(solution)/shard_map/ppermute | solution.py:244
  72.2 6.9 %collective-permute-done.7 = bf16[64,2048]{1,0:T(8,128)(2,1)S(1)} collective-permute-done((bf16[64,2048]{1,0:T(8,128)(2,1)S(1)}, bf16[64,2048]{1,0:T(8,128)(2,1)S(1)}, u32[]{:S(2)}, u32[]{:S(2)}) %collective-permute-start.7) | collective-permute-done | bytes 262176 | tf_op jit(solution)/shard_map/ppermute | solution.py:244
  79.7 7.2 %collective-permute-done.15 = bf16[64,2048]{1,0:T(8,128)(2,1)S(1)} collective-permute-done((bf16[64,2048]{1,0:T(8,128)(2,1)S(1)}, bf16[64,2048]{1,0:T(8,128)(2,1)S(1)}, u32[]{:S(2)}, u32[]{:S(2)}) %collective-permute-start.15) | collective-permute-done | bytes 262176 | tf_op jit(solution)/shard_map/ppermute | solution.py:244
  88.0 6.2 %collective-permute-done.16 = bf16[64,2048]{1,0:T(8,128)(2,1)S(1)} collective-permute-done((bf16[64,2048]{1,0:T(8,128)(2,1)S(1)}, bf16[64,2048]{1,0:T(8,128)(2,1)S(1)}, u32[]{:S(2)}, u32[]{:S(2)}) %collective-permute-start.16) | collective-permute-done | bytes 262176 | tf_op jit(solution)/shard_map/ppermute | solution.py:244
  98.7 8.5 %collective-permute-done.18.refs_14_ = bf16[128,2048]{1,0:T(8,128)(2,1)S(1)} collective-permute-done((bf16[128,2048]{1,0:T(8,128)(2,1)S(1)}, bf16[128,2048]{1,0:T(8,128)(2,1)S(1)}, u32[]{:S(2)}, u32[]{:S(2)}) %collective-permute-start.18) | collective-permute-done | bytes 524320 | tf_op jit(solution)/shard_map/ppermute | solution.py:244
  111.3 7.1 %collective-permute-done.10.refs_7_ = bf16[128,2048]{1,0:T(8,128)(2,1)S(1)} collective-permute-done((bf16[128,2048]{1,0:T(8,128)(2,1)S(1)}, bf16[128,2048]{1,0:T(8,128)(2,1)S(1)}, u32[]{:S(2)}, u32[]{:S(2)}) %collective-permute-start.10) | collective-permute-done | bytes 524320 | tf_op jit(solution)/shard_map/ppermute | solution.py:244
  118.5 4.0 %collective-permute-done.20.refs_16_ = bf16[128,2048]{1,0:T(8,128)(2,1)S(1)} collective-permute-done((bf16[128,2048]{1,0:T(8,128)(2,1)S(1)}, bf16[128,2048]{1,0:T(8,128)(2,1)S(1)}, u32[]{:S(2)}, u32[]{:S(2)}) %collective-permute-start.20) | collective-permute-done | bytes 524320 | tf_op jit(solution)/shard_map/ppermute | solution.py:244
  122.5 3.5 %collective-permute-done.19.refs_15_ = bf16[128,2048]{1,0:T(8,128)(2,1)S(1)} collective-permute-done((bf16[128,2048]{1,0:T(8,128)(2,1)S(1)}, bf16[128,2048]{1,0:T(8,128)(2,1)S(1)}, u32[]{:S(2)}, u32[]{:S(2)}) %collective-permute-start.19) | collective-permute-done | bytes 524320 | tf_op jit(solution)/shard_map/ppermute | solution.py:244
  128.7 35.3 %shard_map.180 = (bf16[128,2048]{1,0:T(8,128)(2,1)}, bf16[128,2048]{1,0:T(8,128)(2,1)}, bf16[128,2048]{1,0:T(8,128)(2,1)}, bf16[128,2048]{1,0:T(8,128)(2,1)}, bf...) custom-call(s32[2]{0:T(128)} %pad_add_fusion.place.refs_0_, ...), custom_call_target="tpu_custom_call" | custom-call | flops 20000000000 | bytes 60000000 | tf_op jit(solution)/shard_map/pallas_call | solution.py:596
  172.4 8.0 %collective-permute-done.26 = bf16[128,2048]{1,0:T(8,128)(2,1)S(1)} collective-permute-done((bf16[128,2048]{1,0:T(8,128)(2,1)S(1)}, bf16[128,2048]{1,0:T(8,128)(2,1)S(1)}, u32[]{:S(2)}, u32[]{:S(2)}) %collective-permute-start.26) | collective-permute-done | bytes 524320 | tf_op jit(solution)/shard_map/ppermute | solution.py:244
  183.4 9.9 %collective-permute-done.39 = bf16[128,2048]{1,0:T(8,128)(2,1)S(1)} collective-permute-done((bf16[128,2048]{1,0:T(8,128)(2,1)S(1)}, bf16[128,2048]{1,0:T(8,128)(2,1)S(1)}, u32[]{:S(2)}, u32[]{:S(2)}) %collective-permute-start.39) | collective-permute-done | bytes 524320 | tf_op jit(solution)/shard_map/ppermute | solution.py:244
  195.3 4.0 %collective-permute-done.31 = bf16[128,2048]{1,0:T(8,128)(2,1)S(1)} collective-permute-done((bf16[128,2048]{1,0:T(8,128)(2,1)S(1)}, bf16[128,2048]{1,0:T(8,128)(2,1)S(1)}, u32[]{:S(2)}, u32[]{:S(2)}) %collective-permute-start.31) | collective-permute-done | bytes 524320 | tf_op jit(solution)/shard_map/ppermute | solution.py:244
  201.0 3.9 %collective-permute-done.40 = bf16[128,2048]{1,0:T(8,128)(2,1)S(1)} collective-permute-done((bf16[128,2048]{1,0:T(8,128)(2,1)S(1)}, bf16[128,2048]{1,0:T(8,128)(2,1)S(1)}, u32[]{:S(2)}, u32[]{:S(2)}) %collective-permute-start.40) | collective-permute-done | bytes 524320 | tf_op jit(solution)/shard_map/ppermute | solution.py:244
  208.5 7.9 %collective-permute-done.41 = bf16[64,2048]{1,0:T(8,128)(2,1)S(1)} collective-permute-done((bf16[64,2048]{1,0:T(8,128)(2,1)S(1)}, bf16[64,2048]{1,0:T(8,128)(2,1)S(1)}, u32[]{:S(2)}, u32[]{:S(2)}) %collective-permute-start.41) | collective-permute-done | bytes 262176 | tf_op jit(solution)/shard_map/ppermute | solution.py:244
  216.4 10.3 %collective-permute-done.42 = bf16[64,2048]{1,0:T(8,128)(2,1)S(1)} collective-permute-done((bf16[64,2048]{1,0:T(8,128)(2,1)S(1)}, bf16[64,2048]{1,0:T(8,128)(2,1)S(1)}, u32[]{:S(2)}, u32[]{:S(2)}) %collective-permute-start.42) | collective-permute-done | bytes 262176 | tf_op jit(solution)/shard_map/ppermute | solution.py:244
  (166 shorter events, 54.7 us)
Async XLA Ops:
  3.5 17.2 %collective-permute-start = (bf16[256,1024]{1,0:T(8,128)(2,1)}, bf16[256,1024]{1,0:T(8,128)(2,1)}, u32[]{:S(2)}, u32[]{:S(2)}) collective-permute-start(bf16[256,1024]{1,0:T(8,128)(2,1)} %get-tuple-element.42.own), channel_id=1, source_target_pairs={{0,8},{4,12},{8,16},{12,20},{16,24},{20,28},{1,9},{5,13},{9,17},{1... | collective-permute-start | bytes 1572872 | tf_op jit(solution)/shard_map/ppermute | solution.py:693
  11.5 13.3 %all-to-all-start = ((f32[8,1,3072]{2,1,0:T(1,128)}), f32[8,1,3072]{2,1,0:T(1,128)S(1)}, u32[]{:S(2)}, u32[]{:S(2)}) async-start(f32[8,1,3072]{2,1,0:T(1,128)} %reshape.26), calls=%async_computation | async-start | bytes 196608 | tf_op jit(solution)/shard_map/all_to_all | solution.py:637
  20.7 23.9 %collective-permute-start.4 = (bf16[256,1024]{1,0:T(8,128)(2,1)}, bf16[256,1024]{1,0:T(8,128)(2,1)}, u32[]{:S(2)}, u32[]{:S(2)}) collective-permute-start(bf16[256,1024]{1,0:T(8,128)(2,1)} %get-tuple-element.42.own), channel_id=1, source_target_pairs={{0,4},{8,12},{16,20},{24,28},{1,5},{9,13},{17,21},{25,29},{2,6},{1... | collective-permute-start | bytes 1572872 | tf_op jit(solution)/shard_map/ppermute | solution.py:693
  26.4 23.6 %collective-permute-start.3 = (bf16[256,1024]{1,0:T(8,128)(2,1)}, bf16[256,1024]{1,0:T(8,128)(2,1)S(1)}, u32[]{:S(2)}, u32[]{:S(2)}) collective-permute-start(bf16[256,1024]{1,0:T(8,128)(2,1)} %collective-permute-done.near_z), channel_id=1, source_target_pairs={{4,8},{12,16},{20,24},{5,9},{13,17},{21,25},{6,10},{14,18},{22,26}... | collective-permute-start | bytes 1572872 | tf_op jit(solution)/shard_map/ppermute | solution.py:693
  27.1 22.9 %collective-permute-start.2 = (bf16[256,1024]{1,0:T(8,128)(2,1)}, bf16[256,1024]{1,0:T(8,128)(2,1)S(1)}, u32[]{:S(2)}, u32[]{:S(2)}) collective-permute-start(bf16[256,1024]{1,0:T(8,128)(2,1)} %collective-permute-done.near_z), channel_id=1, source_target_pairs={{0,8},{4,12},{8,16},{12,20},{16,24},{20,28},{1,9},{5,13},{9,17},{1... | collective-permute-start | bytes 1572872 | tf_op jit(solution)/shard_map/ppermute | solution.py:693
  32.2 17.8 %collective-permute-start.1 = (bf16[256,1024]{1,0:T(8,128)(2,1)}, bf16[256,1024]{1,0:T(8,128)(2,1)}, u32[]{:S(2)}, u32[]{:S(2)}) collective-permute-start(bf16[256,1024]{1,0:T(8,128)(2,1)} %collective-permute-done.near_z), channel_id=1, source_target_pairs={{0,4},{4,0},{8,12},{12,8},{16,20},{20,16},{24,28},{28,24},{1,5},{5... | collective-permute-start | bytes 1572872 | tf_op jit(solution)/shard_map/ppermute | solution.py:693
  94.2 13.0 %collective-permute-start.18 = (bf16[128,2048]{1,0:T(8,128)(2,1)S(1)}, bf16[128,2048]{1,0:T(8,128)(2,1)S(1)}, u32[]{:S(2)}, u32[]{:S(2)}) collective-permute-start(bf16[128,2048]{1,0:T(8,128)(2,1)S(1)} %constant_dynamic-update-slice_fusion.refs_12_), channel_id=1, source_target_pairs={{0,4},{1,3},{2,6},{3,1},{4,0},{5,7},{6,2},{7,5},{8,12},{9,11},{10,... | collective-permute-start | bytes 1572872 | tf_op jit(solution)/shard_map/ppermute | solution.py:244
  94.8 14.0 %collective-permute-start.17 = (bf16[128,2048]{1,0:T(8,128)(2,1)S(1)}, bf16[128,2048]{1,0:T(8,128)(2,1)S(1)}, u32[]{:S(2)}, u32[]{:S(2)}) collective-permute-start(bf16[128,2048]{1,0:T(8,128)(2,1)S(1)} %constant_dynamic-update-slice_fusion.refs_12_), channel_id=1, source_target_pairs={{0,1},{1,0},{2,3},{3,2},{4,5},{5,4},{6,7},{7,6},{8,9},{9,8},{10,11... | collective-permute-start | bytes 1572872 | tf_op jit(solution)/shard_map/ppermute | solution.py:244
  96.5 12.6 %collective-permute-start.12 = (bf16[128,2048]{1,0:T(8,128)(2,1)S(1)}, bf16[128,2048]{1,0:T(8,128)(2,1)S(1)}, u32[]{:S(2)}, u32[]{:S(2)}) collective-permute-start(bf16[128,2048]{1,0:T(8,128)(2,1)S(1)} %collective-permute-done.9.refs_6_), channel_id=1, source_target_pairs={{0,1},{1,0},{2,3},{3,2},{4,5},{5,4},{6,7},{7,6},{8,9},{9,8},{10,11... | collective-permute-start | bytes 1572872 | tf_op jit(solution)/shard_map/ppermute | solution.py:244
  96.5 14.8 %collective-permute-start.11 = (bf16[128,2048]{1,0:T(8,128)(2,1)S(1)}, bf16[128,2048]{1,0:T(8,128)(2,1)S(1)}, u32[]{:S(2)}, u32[]{:S(2)}) collective-permute-start(bf16[128,2048]{1,0:T(8,128)(2,1)S(1)} %collective-permute-done.9.refs_6_), channel_id=1, source_target_pairs={{0,2},{1,5},{2,0},{3,7},{4,6},{5,1},{6,4},{7,3},{8,10},{9,13},{10,... | collective-permute-start | bytes 1572872 | tf_op jit(solution)/shard_map/ppermute | solution.py:244
  98.0 20.4 %collective-permute-start.10 = (bf16[128,2048]{1,0:T(8,128)(2,1)S(1)}, bf16[128,2048]{1,0:T(8,128)(2,1)S(1)}, u32[]{:S(2)}, u32[]{:S(2)}) collective-permute-start(bf16[128,2048]{1,0:T(8,128)(2,1)S(1)} %collective-permute-done.8.refs_5_), channel_id=1, source_target_pairs={{0,4},{1,3},{2,6},{3,1},{4,0},{5,7},{6,2},{7,5},{8,12},{9,11},{10,... | collective-permute-start | bytes 1572872 | tf_op jit(solution)/shard_map/ppermute | solution.py:244
  107.2 15.2 %collective-permute-start.20 = (bf16[128,2048]{1,0:T(8,128)(2,1)S(1)}, bf16[128,2048]{1,0:T(8,128)(2,1)S(1)}, u32[]{:S(2)}, u32[]{:S(2)}) collective-permute-start(bf16[128,2048]{1,0:T(8,128)(2,1)S(1)} %collective-permute-done.18.refs_14_), channel_id=1, source_target_pairs={{0,2},{1,5},{2,0},{3,7},{4,6},{5,1},{6,4},{7,3},{8,10},{9,13},{10,... | collective-permute-start | bytes 1572872 | tf_op jit(solution)/shard_map/ppermute | solution.py:244
  108.7 17.2 %collective-permute-start.19 = (bf16[128,2048]{1,0:T(8,128)(2,1)S(1)}, bf16[128,2048]{1,0:T(8,128)(2,1)S(1)}, u32[]{:S(2)}, u32[]{:S(2)}) collective-permute-start(bf16[128,2048]{1,0:T(8,128)(2,1)S(1)} %collective-permute-done.17.refs_13_), channel_id=1, source_target_pairs={{0,4},{1,3},{2,6},{3,1},{4,0},{5,7},{6,2},{7,5},{8,12},{9,11},{10,... | collective-permute-start | bytes 1572872 | tf_op jit(solution)/shard_map/ppermute | solution.py:244
  109.1 16.8 %collective-permute-start.21 = (bf16[128,2048]{1,0:T(8,128)(2,1)S(1)}, bf16[128,2048]{1,0:T(8,128)(2,1)S(1)}, u32[]{:S(2)}, u32[]{:S(2)}) collective-permute-start(bf16[128,2048]{1,0:T(8,128)(2,1)S(1)} %collective-permute-done.18.refs_14_), channel_id=1, source_target_pairs={{0,1},{1,0},{2,3},{3,2},{4,5},{5,4},{6,7},{7,6},{8,9},{9,8},{10,11... | collective-permute-start | bytes 1572872 | tf_op jit(solution)/shard_map/ppermute | solution.py:244
  111.3 14.6 %collective-permute-start.14 = (bf16[128,2048]{1,0:T(8,128)(2,1)S(1)}, bf16[128,2048]{1,0:T(8,128)(2,1)S(1)}, u32[]{:S(2)}, u32[]{:S(2)}) collective-permute-start(bf16[128,2048]{1,0:T(8,128)(2,1)S(1)} %collective-permute-done.11.refs_8_), channel_id=1, source_target_pairs={{0,1},{1,0},{2,3},{3,2},{4,5},{5,4},{6,7},{7,6},{8,9},{9,8},{10,11... | collective-permute-start | bytes 1572872 | tf_op jit(solution)/shard_map/ppermute | solution.py:244
  165.1 17.7 %collective-permute-start.37 = (bf16[128,2048]{1,0:T(8,128)(2,1)}, bf16[128,2048]{1,0:T(8,128)(2,1)S(1)}, u32[]{:S(2)}, u32[]{:S(2)}) collective-permute-start(bf16[128,2048]{1,0:T(8,128)(2,1)} %get-tuple-element.64), channel_id=1, source_target_pairs={{0,1},{1,0},{2,3},{3,2},{4,5},{5,4},{6,7},{7,6},{8,9},{9,8},{10,11... | collective-permute-start | bytes 1572872 | tf_op jit(solution)/shard_map/ppermute | solution.py:244
  167.6 12.9 %collective-permute-start.26 = (bf16[128,2048]{1,0:T(8,128)(2,1)S(1)}, bf16[128,2048]{1,0:T(8,128)(2,1)S(1)}, u32[]{:S(2)}, u32[]{:S(2)}) collective-permute-start(bf16[128,2048]{1,0:T(8,128)(2,1)S(1)} %add_convert_fusion.6), channel_id=1, source_target_pairs={{0,4},{1,3},{2,6},{3,1},{4,0},{5,7},{6,2},{7,5},{8,12},{9,11},{10,... | collective-permute-start | bytes 1572872 | tf_op jit(solution)/shard_map/ppermute | solution.py:244
  169.9 12.1 %collective-permute-start.30 = (bf16[128,2048]{1,0:T(8,128)(2,1)S(1)}, bf16[128,2048]{1,0:T(8,128)(2,1)S(1)}, u32[]{:S(2)}, u32[]{:S(2)}) collective-permute-start(bf16[128,2048]{1,0:T(8,128)(2,1)S(1)} %add_convert_fusion.5), channel_id=1, source_target_pairs={{0,2},{1,5},{2,0},{3,7},{4,6},{5,1},{6,4},{7,3},{8,10},{9,13},{10,... | collective-permute-start | bytes 1572872 | tf_op jit(solution)/shard_map/ppermute | solution.py:244
  171.6 21.7 %collective-permute-start.39 = (bf16[128,2048]{1,0:T(8,128)(2,1)S(1)}, bf16[128,2048]{1,0:T(8,128)(2,1)S(1)}, u32[]{:S(2)}, u32[]{:S(2)}) collective-permute-start(bf16[128,2048]{1,0:T(8,128)(2,1)S(1)} %add_convert_fusion.2), channel_id=1, source_target_pairs={{0,2},{1,5},{2,0},{3,7},{4,6},{5,1},{6,4},{7,3},{8,10},{9,13},{10,... | collective-permute-start | bytes 1572872 | tf_op jit(solution)/shard_map/ppermute | solution.py:244
  172.3 21.2 %collective-permute-start.24 = (bf16[128,2048]{1,0:T(8,128)(2,1)S(1)}, bf16[128,2048]{1,0:T(8,128)(2,1)S(1)}, u32[]{:S(2)}, u32[]{:S(2)}) collective-permute-start(bf16[128,2048]{1,0:T(8,128)(2,1)S(1)} %copy-done.17), channel_id=1, source_target_pairs={{0,1},{1,0},{2,3},{3,2},{4,5},{5,4},{6,7},{7,6},{8,9},{9,8},{10,11... | collective-permute-start | bytes 1572872 | tf_op jit(solution)/shard_map/ppermute | solution.py:244
  180.4 14.1 %collective-permute-start.35 = (bf16[128,2048]{1,0:T(8,128)(2,1)S(1)}, bf16[128,2048]{1,0:T(8,128)(2,1)S(1)}, u32[]{:S(2)}, u32[]{:S(2)}) collective-permute-start(bf16[128,2048]{1,0:T(8,128)(2,1)S(1)} %add_convert_fusion.3), channel_id=1, source_target_pairs={{0,4},{1,3},{2,6},{3,1},{4,0},{5,7},{6,2},{7,5},{8,12},{9,11},{10,... | collective-permute-start | bytes 1572872 | tf_op jit(solution)/shard_map/ppermute | solution.py:244
  182.0 13.3 %collective-permute-start.27 = (bf16[128,2048]{1,0:T(8,128)(2,1)S(1)}, bf16[128,2048]{1,0:T(8,128)(2,1)S(1)}, u32[]{:S(2)}, u32[]{:S(2)}) collective-permute-start(bf16[128,2048]{1,0:T(8,128)(2,1)S(1)} %collective-permute-done.26), channel_id=1, source_target_pairs={{0,1},{1,0},{2,3},{3,2},{4,5},{5,4},{6,7},{7,6},{8,9},{9,8},{10,11... | collective-permute-start | bytes 1572872 | tf_op jit(solution)/shard_map/ppermute | solution.py:244
  182.8 16.5 %collective-permute-start.31 = (bf16[128,2048]{1,0:T(8,128)(2,1)S(1)}, bf16[128,2048]{1,0:T(8,128)(2,1)S(1)}, u32[]{:S(2)}, u32[]{:S(2)}) collective-permute-start(bf16[128,2048]{1,0:T(8,128)(2,1)S(1)} %add_convert_fusion.4), channel_id=1, source_target_pairs={{0,4},{1,3},{2,6},{3,1},{4,0},{5,7},{6,2},{7,5},{8,12},{9,11},{10,... | collective-permute-start | bytes 1572872 | tf_op jit(solution)/shard_map/ppermute | solution.py:244
  208.5 18.2 %collective-permute-start.42 = (bf16[64,2048]{1,0:T(8,128)(2,1)S(1)}, bf16[64,2048]{1,0:T(8,128)(2,1)S(1)}, u32[]{:S(2)}, u32[]{:S(2)}) collective-permute-start(bf16[64,2048]{1,0:T(8,128)(2,1)S(1)} %get-tuple-element.71), channel_id=1, source_target_pairs={{0,8},{1,9},{2,10},{3,11},{4,12},{5,13},{6,14},{7,15},{8,24},{9,25... | collective-permute-start | bytes 786440 | tf_op jit(solution)/shard_map/ppermute | solution.py:244
  (52 other events, 568.1 us)
